TPU v7x, 256 devices: a whole 4x4x8 slice. The times are simulated.
256 devices in a mesh: seq: 32 (over z, x_lo, core), head: 8 (over x_hi, y).
Axes of the slice: x: 4 (x_hi: 2, x_lo: 2; x = x_hi * 2 + x_lo), y: 4, z: 8, core: 2. Of those that a mesh axis runs over, the one named last changes fastest.
Arguments:
- self_queries: bfloat16 [8192, 5120], P(('seq', 'head')), may hold values from -8 to 8
- self_keys: bfloat16 [8192, 5120], P(('seq', 'head')), may hold values from -8 to 8
- self_values: bfloat16 [8192, 5120], P(('seq', 'head')), may hold values from -6 to 6
- text_queries: bfloat16 [8192, 5120], P(('seq', 'head')), may hold values from -8 to 8
- text_context: bfloat16 [32, 2, 512, 5120], P('seq', None, None, 'head'), may hold values from -8 to 8
- sample: int32 [32], replicated, may hold values from 0 to 31, each once
- text_lengths: int32 [32], replicated, may hold values from 128 to 512
- timestep: int32 [32], replicated, may hold values from 0 to 49
- time_gates: float32 [50, 5120], replicated, may hold values from 0.2 to 1.8
Outputs:
- self_attended: bfloat16 [8192, 5120], P(('seq', 'head'))
- cross_attended: bfloat16 [8192, 5120], P(('seq', 'head'))
Inputs may be any that keep to these rules, and one draw needn't show every extreme that they name: Each index of a loaded sample appears once.
All inputs are finite; a program needn't handle non-finite values.
Results may differ from a plain program's by a relative error of at most 0.007.
Values may be sent and summed in bfloat16 or wider, within the bound.
No kernel may reach another device: no remote copies, remote signals or barrier semaphores. Data moves between devices by JAX's collectives and lax.ppermute only.
A program may use at most 192 MiB of HBM per device.

v0:
```python
import math

import jax
import jax.numpy as jnp
from jax import lax
from jax.sharding import PartitionSpec as P

HD = 128


def broadcast(block, axis, source):
    block = jnp.where(lax.axis_index(axis) == source, block, jnp.zeros_like(block))
    return lax.psum(block, axis)


def cross_attend(query_rows, key_rows, value_rows, length):
    row_count, width = query_rows.shape
    local_heads = width // HD
    factor = 1.0 / math.sqrt(HD)
    queries = query_rows.reshape(row_count, local_heads, HD)
    keyed = key_rows.reshape(key_rows.shape[0], local_heads, HD)
    valued = value_rows.reshape(value_rows.shape[0], local_heads, HD)
    scores = jnp.einsum("thd,nhd->htn", queries, keyed, preferred_element_type=jnp.float32) * factor
    valid_keys = jnp.arange(key_rows.shape[0]) < length
    scores = jnp.where(valid_keys[None, None, :], scores, jnp.float32(-1e30))
    maxima = jnp.max(scores, axis=-1, keepdims=True)
    weights = jnp.exp(scores - maxima)
    totals = jnp.sum(weights, axis=-1, keepdims=True)
    summed = jnp.einsum(
        "htn,nhd->htd", weights.astype(jnp.bfloat16), valued, preferred_element_type=jnp.float32
    )
    result = (summed / totals).astype(jnp.bfloat16)
    return result.transpose(1, 0, 2).reshape(row_count, width)


def on_device(
    self_queries,
    self_keys,
    self_values,
    text_queries,
    text_context,
    sample,
    text_lengths,
    timestep,
    time_gates,
):
    factor = 1.0 / math.sqrt(HD)
    chosen = sample[0]
    query_heads, key_heads, value_heads = (
        lax.all_to_all(self_queries, "head", split_axis=1, concat_axis=0, tiled=True),
        lax.all_to_all(self_keys, "head", split_axis=1, concat_axis=0, tiled=True),
        lax.all_to_all(self_values, "head", split_axis=1, concat_axis=0, tiled=True),
    )
    owned_text = broadcast(text_context, "seq", chosen)
    length = lax.dynamic_index_in_dim(text_lengths, chosen, 0, keepdims=False)
    rows_all, width = query_heads.shape
    local_heads = width // HD
    queries = query_heads.reshape(rows_all, local_heads, HD)
    pieces = (
        lax.all_gather(key_heads, "seq", axis=0, tiled=True),
        lax.all_gather(value_heads, "seq", axis=0, tiled=True),
    )
    maxima = jnp.full((local_heads, rows_all), -1e30, jnp.float32)
    key_rows = pieces[0].reshape(pieces[0].shape[0], local_heads, HD)
    value_rows = pieces[1].reshape(pieces[1].shape[0], local_heads, HD)
    scores = (
        jnp.einsum("thd,nhd->htn", queries, key_rows, preferred_element_type=jnp.float32) * factor
    )
    updated = jnp.maximum(maxima, jnp.max(scores, axis=-1))
    weights = jnp.exp(scores - updated[..., None])
    totals = jnp.sum(weights, axis=-1)
    accumulated = jnp.einsum(
        "htn,nhd->htd", weights.astype(jnp.bfloat16), value_rows, preferred_element_type=jnp.float32
    )
    maxima, totals, accumulated = (updated, totals, accumulated)
    attended = (
        (accumulated / totals[..., None])
        .astype(jnp.bfloat16)
        .transpose(1, 0, 2)
        .reshape(rows_all, width)
    )
    attended_rows = lax.all_to_all(attended, "head", split_axis=0, concat_axis=1, tiled=True)
    full_text = lax.all_gather(owned_text, "head", axis=3, tiled=True)
    cross_attended = cross_attend(text_queries, full_text[0, 0], full_text[0, 1], length)
    step_index = lax.dynamic_index_in_dim(timestep, chosen, 0, keepdims=False)
    step_rows = jnp.arange(time_gates.shape[0])[:, None] == step_index
    gate_row = jnp.sum(jnp.where(step_rows, time_gates, jnp.float32(0.0)), axis=0)
    self_attended = (gate_row[None, :] * attended_rows.astype(jnp.float32)).astype(jnp.bfloat16)
    return (self_attended, cross_attended)


def solution(mesh):
    in_specs = (
        P(("seq", "head"), None),
        P(("seq", "head"), None),
        P(("seq", "head"), None),
        P(("seq", "head"), None),
        P("seq", None, None, "head"),
        P(),
        P(),
        P(),
        P(),
    )
    out_specs = (P(("seq", "head"), None), P(("seq", "head"), None))
    return jax.shard_map(
        on_device, mesh=mesh, in_specs=in_specs, out_specs=out_specs, check_vma=False
    )
```

profile of v0, /device:TPU:8, one launch (start us, length us, event | category | flops | bytes accessed | tf_op | source)
XLA Modules:
  0.0 592.9 jit_solution(12627847187982399709)
XLA Ops:
  7.3 1.7 copy.49
  9.7 1.2 broadcast_select_fusion
  11.0 230.8 %all-reduce.2.cloned.1.call-done = bf16[1,2,512,640]{2,3,1,0:T(8,128)(2,1)} async-done(((bf16[1,2,512,640]{2,3,1,0:T(8,128)(2,1)}), bf16[1,2,512,640]{2,3,1,0:T(8,128)(2,1)}) %all-reduce.2.cloned.1.call-update) | async-done | bytes 1310736 | tf_op jit(solution)/shard_map/psum | solution.py:13
  241.9 15.4 %all_to_all.67 = bf16[32,8,640]{2,0,1:T(8,128)(2,1)} all-to-all(bf16[32,8,640]{2,0,1:T(8,128)(2,1)S(1)} %bitcast.91), channel_id=1, replica_groups=mesh['seq'=32,'head'=8] {'head'}, dimensions={1} | all-to-all | bytes 655360 | tf_op jit(solution)/shard_map/all_to_all | solution.py:51
  257.5 16.5 %all_to_all.68 = bf16[32,8,640]{2,0,1:T(8,128)(2,1)} all-to-all(bf16[32,8,640]{2,0,1:T(8,128)(2,1)S(1)} %bitcast.92), channel_id=1, replica_groups=mesh['seq'=32,'head'=8] {'head'}, dimensions={1} | all-to-all | bytes 655360 | tf_op jit(solution)/shard_map/all_to_all | solution.py:52
  274.8 4.8 all-to-all-start
  282.5 4.5 all-to-all-done
  287.3 92.6 %all-gather.8.cloned.1.call-done = bf16[1,2,512,5120]{2,3,1,0:T(8,128)(2,1)} async-done(((bf16[1,2,512,640]{2,3,1,0:T(8,128)(2,1)}), bf16[1,2,512,5120]{2,3,1,0:T(8,128)(2,1)}) %all-gather.8.cloned.1.call-update) | async-done | bytes 10485776 | tf_op jit(solution)/shard_map/all_gather | solution.py:83
  379.9 8.6 %fusion.44 = (bf16[1,1,512,5120]{2,3,1,0:T(8,128)(2,1)}, bf16[1,1,512,5120]{2,3,1,0:T(8,128)(2,1)}) fusion(bf16[1,2,512,5120]{2,3,1,0:T(8,128)(2,1)} %all-gather.8.cloned.1.call-done), kind=kLoop, calls=%fused_computation.44 | loop fusion | bytes 20971520 | tf_op jit(solution)/shard_map/slice | solution.py:84
  388.5 3.5 bitcast_reduce_fusion
  392.0 0.8 fusion.7
  392.8 63.1 %all-gather.4.cloned.1.call-done = bf16[8192,640]{1,0:T(8,128)(2,1)} async-done(((bf16[256,640]{1,0:T(8,128)(2,1)}), bf16[8192,640]{1,0:T(8,128)(2,1)}) %all-gather.4.cloned.1.call-update) | async-done | bytes 10485776 | tf_op jit(solution)/shard_map/all_gather | solution.py:60
  455.9 14.3 %copy.41 = bf16[8192,640]{0,1:T(8,128)(2,1)} copy(bf16[8192,640]{1,0:T(8,128)(2,1)} %all-gather.4.cloned.1.call-done) | data formatting | bytes 20971520 | tf_op jit(solution)/shard_map/all_gather | solution.py:60
  470.2 20.9 %multiply_reduce_fusion = (f32[5,256]{1,0:T(8,128)S(1)}, f32[5,256,8192]{2,1,0:T(8,128)}) fusion(bf16[8192,5,128]{0,2,1:T(8,128)(2,1)} %bitcast.83, bf16[256,5,128]{2,1,0:T(8,128)(2,1)S(1)} %reshape.52), kind=kOutput, calls=%fused_computation.1 | convolution fusion | flops 2705324800 | bytes 52761600 | tf_op jit(solution)/shard_map/thd,nhd->htn/dot_general | solution.py:67
  491.2 17.8 %fusion = f32[5,256]{1,0:T(8,128)S(1)} fusion(f32[5,256,8192]{2,1,0:T(8,128)} %get-tuple-element.5, f32[5,256]{1,0:T(8,128)S(1)} %broadcast_maximum_fusion), kind=kLoop, calls=%fused_computation.2 | loop fusion | flops 31456000 | bytes 41953280 | tf_op jit(solution)/shard_map/reduce_sum | solution.py:71
  509.0 23.3 %all-gather.6.cloned.1.call-done = bf16[8192,640]{1,0:T(8,128)(2,1)} async-done(((bf16[256,640]{1,0:T(8,128)(2,1)}), bf16[8192,640]{1,0:T(8,128)(2,1)}) %all-gather.6.cloned.1.call-update) | async-done | bytes 10485776 | tf_op jit(solution)/shard_map/all_gather | solution.py:61
  532.3 14.3 %copy.45 = bf16[8192,640]{0,1:T(8,128)(2,1)} copy(bf16[8192,640]{1,0:T(8,128)(2,1)} %all-gather.6.cloned.1.call-done) | data formatting | bytes 20971520 | tf_op jit(solution)/shard_map/all_gather | solution.py:61
  546.6 22.6 %fusion.24 = bf16[256,5,128]{2,0,1:T(8,128)(2,1)S(1)} fusion(bf16[8192,5,128]{0,2,1:T(8,128)(2,1)} %bitcast.84, f32[5,256,8192]{2,1,0:T(8,128)} %get-tuple-element.5, f32[5,256]{1,0:T(8,128)S(1)} %broadcast_maximum_fusion, f32[256,5]{0,1:T(8,128)S(1)} %bitcast.97), kind=kOutput, calls=%fused_computation.23 | convolution fusion | flops 2716139520 | bytes 52766720 | tf_op jit(solution)/shard_map/htn,nhd->htd/dot_general | solution.py:72
  569.4 1.1 all_to_all.61
  570.5 7.1 %all-to-all-start.3 = ((bf16[8,32,640]{2,1,0:T(8,128)(2,1)}), bf16[8,32,640]{2,1,0:T(8,128)(2,1)S(1)}, u32[]{:S(2)}, u32[]{:S(2)}) async-start(bf16[8,32,640]{2,1,0:T(8,128)(2,1)} %all_to_all.61), calls=%async_computation.3 | async-start | bytes 655360 | tf_op jit(solution)/shard_map/all_to_all | solution.py:82
  577.7 4.5 fusion.33
  582.2 0.8 copy.78
  583.0 2.5 all-to-all-done.3
  585.6 0.8 multiply_convert_fusion
  (39 shorter events, 4.5 us)
Async XLA Ops:
  7.2 381.4 %copy-start = (bf16[32,5120]{1,0:T(8,128)(2,1)S(1)}, bf16[32,5120]{1,0:T(8,128)(2,1)}, u32[]{:S(2)}) copy-start(bf16[32,5120]{1,0:T(8,128)(2,1)} %param.12) | copy-start | bytes 983044
  7.2 234.7 %copy-start.3 = (bf16[32,5120]{1,0:T(8,128)(2,1)S(1)}, bf16[32,5120]{1,0:T(8,128)(2,1)}, u32[]{:S(2)}) copy-start(bf16[32,5120]{1,0:T(8,128)(2,1)} %param.10) | copy-start | bytes 983044
  7.2 250.3 %copy-start.4 = (bf16[32,5120]{1,0:T(8,128)(2,1)S(1)}, bf16[32,5120]{1,0:T(8,128)(2,1)}, u32[]{:S(2)}) copy-start(bf16[32,5120]{1,0:T(8,128)(2,1)} %param.11) | copy-start | bytes 983044
  7.2 234.6 %all-reduce.2.cloned.1.call-start = ((), (), s32[]{:S(2)}) async-start(), calls=%async_computation.6 | async-start | bytes 2621440 | tf_op jit(solution)/shard_map/psum | solution.py:13
  8.9 270.7 %copy-start.6 = (s32[32]{0:T(128)S(1)}, s32[32]{0:T(128)}, u32[]{:S(2)}) copy-start(s32[32]{0:T(128)} %param.14) | copy-start | bytes 388
  8.9 270.8 %copy-start.7 = (s32[32]{0:T(128)S(1)}, s32[32]{0:T(128)}, u32[]{:S(2)}) copy-start(s32[32]{0:T(128)} %param.15) | copy-start | bytes 388
  9.0 272.0 %copy-start.8 = (s32[32]{0:T(128)S(1)}, s32[32]{0:T(128)}, u32[]{:S(2)}) copy-start(s32[32]{0:T(128)} %param.16) | copy-start | bytes 388
  9.0 273.3 %copy-start.2 = (f32[50,5120]{1,0:T(8,128)S(1)}, f32[50,5120]{1,0:T(8,128)}, u32[]{:S(2)}) copy-start(f32[50,5120]{1,0:T(8,128)} %param.17) | copy-start | bytes 3072004
  10.9 263.1 %copy-start.5 = (bf16[32,5120]{1,0:T(8,128)(2,1)S(1)}, bf16[32,5120]{1,0:T(8,128)(2,1)}, u32[]{:S(2)}) copy-start(bf16[32,5120]{1,0:T(8,128)(2,1)} %param.9) | copy-start | bytes 983044
  10.9 369.0 %all-gather.8.cloned.1.call-start = ((), (), s32[]{:S(2)}) async-start(), calls=%async_computation.7 | async-start | bytes 11796480 | tf_op jit(solution)/shard_map/all_gather | solution.py:83
  241.9 214.1 %all-gather.4.cloned.1.call-start = ((), (), s32[]{:S(2)}) async-start(), calls=%async_computation.4 | async-start | bytes 10813440 | tf_op jit(solution)/shard_map/all_gather | solution.py:60
  257.4 274.9 %all-gather.6.cloned.1.call-start = ((), (), s32[]{:S(2)}) async-start(), calls=%async_computation.5 | async-start | bytes 10813440 | tf_op jit(solution)/shard_map/all_gather | solution.py:61
  274.8 12.1 %all-to-all-start = ((bf16[32,8,640]{2,0,1:T(8,128)(2,1)}), bf16[32,8,640]{2,0,1:T(8,128)(2,1)S(1)}, u32[]{:S(2)}, u32[]{:S(2)}) async-start(bf16[32,8,640]{2,0,1:T(8,128)(2,1)} %bitcast.81), calls=%async_computation | async-start | bytes 655360 | tf_op jit(solution)/shard_map/all_to_all | solution.py:50
  570.5 15.0 %all-to-all-start.3 = ((bf16[8,32,640]{2,1,0:T(8,128)(2,1)}), bf16[8,32,640]{2,1,0:T(8,128)(2,1)S(1)}, u32[]{:S(2)}, u32[]{:S(2)}) async-start(bf16[8,32,640]{2,1,0:T(8,128)(2,1)} %all_to_all.61), calls=%async_computation.3 | async-start | bytes 655360 | tf_op jit(solution)/shard_map/all_to_all | solution.py:82
  577.7 8.7 %copy-start.1 = (bf16[32,5120]{1,0:T(8,128)(2,1)S(1)}, bf16[32,5120]{1,0:T(8,128)(2,1)}, u32[]{:S(2)}) copy-start(bf16[32,5120]{1,0:T(8,128)(2,1)} %param.12) | copy-start | bytes 983044
Sparse Core Ops, SparseCore 0:
  11.1 230.7 all-reduce.1
  244.8 135.1 all-gather.7
  381.9 73.9 all-gather.3
  457.8 74.4 all-gather.5
where the time goes:
time: 595 us; the launch traced here: 593 us
  waiting for transfers between devices  417 us (70%)
  matrix products  51.5 us (9%)
  local copies, waits for them, and re-layouts  43.5 us (7%)
  blocking collectives  32 us (5%)
  other arithmetic  22 us (4%)
  between operations  14.8 us (2%)
  starting transfers between devices  12.1 us (2%)
    psum x1, waiting for transfers between devices, broadcast(): return lax.psum(block, axis)  231 us
    all_gather x1, waiting for transfers between devices, on_device(): full_text = lax.all_gather(owned_text, 'head', axis=3, tiled=True)  92.6 us
    all_gather x1, waiting for transfers between devices, on_device(): lax.all_gather(key_heads, 'seq', axis=0, tiled=True)  63.1 us
    all_gather x1, waiting for transfers between devices, on_device(): lax.all_gather(value_heads, 'seq', axis=0, tiled=True)  23.3 us
    dot_general x1, matrix products, on_device(): jnp.einsum('htn,nhd->htd', weights.astype(jnp.bfloat16), value_rows, pref...  22.6 us
    dot_general x1, matrix products, on_device(): jnp.einsum('thd,nhd->htn', queries, key_rows, preferred_element_type=jnp....  20.9 us
    reduce_sum x1, other arithmetic, on_device(): totals = jnp.sum(weights, axis=-1)  17.8 us
    all_to_all x1, blocking collectives, on_device(): lax.all_to_all(self_values, 'head', split_axis=1, concat_axis=0, tiled=True)  16.5 us
  transfers between devices with their start and end apart: 6, of which 6 were waited for; matrix products, arithmetic and copies ran while one was open for 13% of the time, Pallas kernels for 0%

commit v1 on v0

v1 whole, which is shorter than its diff:
```python
import functools
import math

import jax
import jax.numpy as jnp
from jax import lax
from jax.experimental import pallas as pl
from jax.experimental.pallas import tpu as pltpu
from jax.sharding import Mesh, PartitionSpec as P

AXES = ("z", "xl", "core", "xh", "y")
SIZES = (8, 2, 2, 2, 4)
PLANE = ("xl", "core", "xh", "y")

HD = 128
ROWS = 32
GROUPS = 8
SPLIT = 4
PEERS = GROUPS * SPLIT
PLANE_ROWS = PEERS * ROWS
TEXT = 512
SCALE = math.log2(math.e) / math.sqrt(HD)
F32 = jnp.float32
BF16 = jnp.bfloat16
VMEM_LIMIT = 48 * 1024 * 1024


def call(kernel, out_shape, cost=None, **kwargs):
    return pl.pallas_call(
        kernel,
        out_shape=out_shape,
        cost_estimate=cost,
        compiler_params=pltpu.CompilerParams(vmem_limit_bytes=VMEM_LIMIT),
        **kwargs,
    )


def head_columns(head):
    return slice(head * HD, (head + 1) * HD)


def pack_pairs_kernel(keys_ref, values_ref, out_ref):
    quarter = ROWS // SPLIT
    for j in range(GROUPS):
        fifth = head_columns(5 * j + 4)
        key_rows = keys_ref[:, fifth].astype(F32)
        value_rows = values_ref[:, fifth].astype(F32)
        for i in range(SPLIT):
            to = i * GROUPS + j
            own = head_columns(5 * j + i)
            out_ref[to, 0:32, :] = keys_ref[:, own]
            out_ref[to, 32:64, :] = values_ref[:, own]
            part = slice(i * quarter, (i + 1) * quarter)
            out_ref[to, 64:80, :] = jnp.concatenate([key_rows[part], value_rows[part]]).astype(BF16)


def pack_queries_kernel(queries_ref, text_queries_ref, out_ref):
    for j in range(GROUPS):
        for i in range(SPLIT):
            to = i * GROUPS + j
            own, fifth = head_columns(5 * j + i), head_columns(5 * j + 4)
            out_ref[to, 0:32, :] = queries_ref[:, own]
            out_ref[to, 32:64, :] = queries_ref[:, fifth]
            out_ref[to, 64:96, :] = text_queries_ref[:, own]
            out_ref[to, 96:128, :] = text_queries_ref[:, fifth]


def pack_text_kernel(core_ref, text_ref, keep_ref, send_ref):
    quarter = TEXT // SPLIT

    def write(ref, core):
        for xl in range(2):
            i = xl * 2 + core
            for kind in range(2):
                base = kind * (TEXT + quarter)
                ref[xl, base : base + TEXT, :] = text_ref[0, kind, :, head_columns(i)]
                ref[xl, base + TEXT : base + TEXT + quarter, :] = text_ref[
                    0, kind, i * quarter : (i + 1) * quarter, head_columns(4)
                ]

    @pl.when(core_ref[0] == 0)
    def _():
        write(keep_ref, 0)
        write(send_ref, 1)

    @pl.when(core_ref[0] != 0)
    def _():
        write(keep_ref, 1)
        write(send_ref, 0)


def scores_of(queries, keys):
    return lax.dot_general(queries, keys, (((1,), (1,)), ((), ())), preferred_element_type=F32)


def attend(queries, keys, values, state):
    scores = jnp.concatenate([scores_of(queries, k) for k in keys], axis=1) if len(keys) > 1 else scores_of(queries, keys[0])
    return fold(scores, values, state)


def fold(scores, values, state):
    top = jnp.max(scores, axis=1, keepdims=True)
    if state is not None:
        top = jnp.maximum(top, state[0])
    weights = jnp.exp2((scores - top) * SCALE)
    total = jnp.sum(weights, axis=1, keepdims=True)
    weights = weights.astype(BF16)
    summed, at = None, 0
    for v in values:
        term = jnp.dot(weights[:, at : at + v.shape[0]], v, preferred_element_type=F32)
        summed = term if summed is None else summed + term
        at += v.shape[0]
    if state is not None:
        shrink = jnp.exp2((state[0] - top) * SCALE)
        total = total + state[1] * shrink
        summed = summed + state[2] * shrink
    return top, total, summed


def write_result(out_ref, whole, part):
    count = out_ref.shape[0]
    out_ref[:, 0:32, :] = (whole[2] / whole[1]).astype(BF16).reshape(count, ROWS, HD)
    out_ref[:, 32:64, :] = (part[2] / part[1]).astype(BF16).reshape(count, ROWS, HD)
    size = part[0] * SCALE + jnp.log2(part[1])
    size = jnp.broadcast_to(size, (count * ROWS, HD))
    high = size.astype(BF16).astype(F32)
    middle = (size - high).astype(BF16).astype(F32)
    low = size - high - middle
    lane = lax.broadcasted_iota(jnp.int32, (count * ROWS, HD), 1)
    row = lax.broadcasted_iota(jnp.int32, (count * ROWS, HD), 0)
    terms = jnp.where(lane < 32, high, jnp.where(lane < 64, middle, low))
    terms = jnp.where((lane % 32 == row % 32) & (lane < 96), terms, 0.0)
    terms = jnp.sum(terms.reshape(count, ROWS, HD), axis=1, keepdims=True)
    out_ref[:, 64:80, :] = jnp.broadcast_to(terms, (count, 16, HD)).astype(BF16)


def self_kernel(shards, first, last, *refs):
    queries_ref, shard_refs, rest = refs[0], refs[1 : 1 + shards], refs[1 + shards :]
    if not first:
        whole_ref, part_ref, stats_ref = rest[:3]
        rest = rest[3:]
    block = queries_ref.shape[0] * ROWS
    keys, values, part_keys, part_values = [], [], [], []
    for ref in shard_refs:
        count = ref.shape[0]
        keys.append(ref[:, 0:32, :].reshape(count * 32, HD))
        values.append(ref[:, 32:64, :].reshape(count * 32, HD))
        quarter = ref[:, 64:80, :].astype(F32)
        part_keys.append(quarter[:, 0:8].reshape(count * 8, HD).astype(BF16))
        part_values.append(quarter[:, 8:16].reshape(count * 8, HD).astype(BF16))
    whole_state = part_state = None
    if not first:
        stats = stats_ref[...]
        whole_state = (stats[:, 0:1], stats[:, 1:2], whole_ref[...])
        part_state = (stats[:, 2:3], stats[:, 3:4], part_ref[...])
    whole = attend(queries_ref[:, 0:32, :].reshape(block, HD), keys, values, whole_state)
    part = attend(queries_ref[:, 32:64, :].reshape(block, HD), part_keys, part_values, part_state)
    if last:
        write_result(rest[0], whole, part)
        return
    whole_out, part_out, stats_out = rest
    whole_out[...] = whole[2]
    part_out[...] = part[2]
    lane = lax.broadcasted_iota(jnp.int32, (block, HD), 1)
    stats_out[...] = jnp.where(
        lane == 0, whole[0], jnp.where(lane == 1, whole[1], jnp.where(lane == 2, part[0], part[1]))
    )


def self_step(queries, shards, state, last=False):
    first = state is None
    senders = 8
    block = senders * ROWS
    steps = PEERS // senders
    state_specs = [pl.BlockSpec((block, HD), lambda g: (g, 0))] * 3
    in_specs = [pl.BlockSpec((senders, 128, HD), lambda g: (g, 0, 0))]
    in_specs += [pl.BlockSpec(s.shape, lambda g: (0, 0, 0)) for s in shards]
    in_specs += [] if first else state_specs
    if last:
        out_shape = jax.ShapeDtypeStruct((PEERS, 80, HD), BF16)
        out_specs = pl.BlockSpec((senders, 80, HD), lambda g: (g, 0, 0))
    else:
        out_shape = [jax.ShapeDtypeStruct((PLANE_ROWS, HD), F32)] * 3
        out_specs = state_specs
    keys = sum(s.shape[0] for s in shards) * 40
    cost = pl.CostEstimate(
        flops=4 * PLANE_ROWS * keys * HD * 2,
        bytes_accessed=keys * HD * 4 + PLANE_ROWS * HD * 16,
        transcendentals=PLANE_ROWS * keys,
    )
    return call(
        functools.partial(self_kernel, len(shards), first, last),
        out_shape,
        cost,
        grid=(steps,),
        in_specs=in_specs,
        out_specs=out_specs,
    )(queries, *shards, *(() if first else state))


def cross_kernel(scalars_ref, queries_ref, text_ref, out_ref):
    length, place = scalars_ref[0], scalars_ref[1]
    quarter = TEXT // SPLIT
    block = queries_ref.shape[0] * ROWS

    def masked(scores, start):
        at = start + lax.broadcasted_iota(jnp.int32, scores.shape, 1)
        return jnp.where(at < length, scores, -1e30)

    whole = fold(
        masked(scores_of(queries_ref[:, 64:96, :].reshape(block, HD), text_ref[0:512, :]), 0),
        [text_ref[640:1152, :]],
        None,
    )
    part = fold(
        masked(scores_of(queries_ref[:, 96:128, :].reshape(block, HD), text_ref[512:640, :]), place * quarter),
        [text_ref[1152:1280, :]],
        None,
    )
    write_result(out_ref, whole, part)


def cross_step(scalars, queries, text):
    senders = 8
    return call(
        cross_kernel,
        jax.ShapeDtypeStruct((PEERS, 80, HD), BF16),
        pl.CostEstimate(
            flops=4 * PLANE_ROWS * 640 * HD * 2, bytes_accessed=2 * 1024 * 1024, transcendentals=PLANE_ROWS * 640
        ),
        grid=(PEERS // senders,),
        in_specs=[
            pl.BlockSpec(memory_space=pltpu.SMEM),
            pl.BlockSpec((senders, 128, HD), lambda g: (g, 0, 0)),
            pl.BlockSpec(text.shape, lambda g: (0, 0)),
        ],
        out_specs=pl.BlockSpec((senders, 80, HD), lambda g: (g, 0, 0)),
    )(scalars, queries, text)


def merged(message_ref, j):
    lane = lax.broadcasted_iota(jnp.int32, (ROWS, HD), 1)
    row = lax.broadcasted_iota(jnp.int32, (ROWS, HD), 0)
    mine = (lane % 32 == row) & (lane < 96)
    sizes = []
    for i in range(SPLIT):
        terms = message_ref[i * GROUPS + j, 64:80, :].astype(F32)[0:1]
        sizes.append(jnp.sum(jnp.where(mine, jnp.broadcast_to(terms, (ROWS, HD)), 0.0), axis=1, keepdims=True))
    top = functools.reduce(jnp.maximum, sizes)
    shares = [jnp.exp2(s - top) for s in sizes]
    summed = sum(
        share * message_ref[i * GROUPS + j, 32:64, :].astype(F32) for i, share in enumerate(shares)
    )
    return (summed / sum(shares)).astype(BF16)


def unpack_kernel(gated, *refs):
    message_ref, out_ref = refs[0], refs[-1]
    for j in range(GROUPS):
        for i in range(SPLIT + 1):
            columns = head_columns(5 * j + i)
            rows = message_ref[i * GROUPS + j, 0:32, :] if i < SPLIT else merged(message_ref, j)
            if gated:
                rows = (refs[1][0:1, columns] * rows.astype(F32)).astype(BF16)
            out_ref[:, columns] = rows


def unpack(message, gate=None):
    operands = [message] if gate is None else [message, gate]
    return call(
        functools.partial(unpack_kernel, gate is not None), jax.ShapeDtypeStruct((ROWS, 40 * HD), BF16)
    )(*operands)


def exchange(messages):
    return lax.all_to_all(messages, PLANE, split_axis=0, concat_axis=0, tiled=True)


def shift(block, by):
    size = SIZES[0]
    return lax.ppermute(block, "z", [(z, (z + by) % size) for z in range(size)])


def pick(block, index):
    return lax.dynamic_index_in_dim(block, index, 0, keepdims=False)


def text_of_sample(text_context, chosen):
    z, xl, core = lax.axis_index("z"), lax.axis_index("xl"), lax.axis_index("core")
    part = jax.ShapeDtypeStruct((2, 1280, HD), BF16)
    keep, send = call(
        pack_text_kernel,
        [part, part],
        in_specs=[pl.BlockSpec(memory_space=pltpu.SMEM), pl.BlockSpec(memory_space=pltpu.VMEM)],
    )(core.reshape(1), text_context)
    got = lax.ppermute(send, "core", [(0, 1), (1, 0)])
    held = jnp.where(chosen % 2 == core, keep, got)
    got = lax.ppermute(pick(held, 1 - xl), "xl", [(0, 1), (1, 0)])
    held = jnp.where(chosen // 2 % 2 == xl, pick(held, xl), got)
    pieces = lax.all_to_all(held.reshape(8, 160, HD), "z", split_axis=0, concat_axis=0, tiled=True)
    piece = pick(pieces, chosen // 4)
    return lax.all_gather(piece, "z", axis=0, tiled=True)


def on_device(
    self_queries,
    self_keys,
    self_values,
    text_queries,
    text_context,
    sample,
    text_lengths,
    timestep,
    time_gates,
):
    chosen = sample[0]
    pairs = call(pack_pairs_kernel, jax.ShapeDtypeStruct((PEERS, 80, HD), BF16))(self_keys, self_values)
    pairs = exchange(pairs)
    queries = call(pack_queries_kernel, jax.ShapeDtypeStruct((PEERS, 128, HD), BF16))(self_queries, text_queries)
    queries, pairs = lax.optimization_barrier((queries, pairs))
    queries = exchange(queries)

    half = PEERS // 2
    own = [pairs[:half], pairs[half:]]
    up = [shift(b, 1) for b in own]
    down = [shift(b, -1) for b in own]
    state = self_step(queries, own, None)
    for _ in range(2):
        up_next = [shift(b, 1) for b in up]
        down_next = [shift(b, -1) for b in down]
        state = self_step(queries, up + down, state)
        up, down = up_next, down_next
    far = [shift(up[0], 1), shift(down[1], -1)]
    state = self_step(queries, up + down, state)
    result = exchange(self_step(queries, far, state, last=True))

    text = text_of_sample(text_context, chosen)
    length = pick(text_lengths, chosen)
    place = lax.axis_index("xl") * 2 + lax.axis_index("core")
    cross = exchange(cross_step(jnp.stack([length, place]), queries, text))
    gate = lax.dynamic_slice_in_dim(time_gates, pick(timestep, chosen), 1, 0)
    return (unpack(result, gate), unpack(cross))


def solution(mesh):
    fine = Mesh(mesh.devices.reshape(SIZES), AXES)
    rows = P(AXES, None)
    in_specs = (rows, rows, rows, rows, P(("z", "xl", "core"), None, None, ("xh", "y")), P(), P(), P(), P())
    return jax.shard_map(on_device, mesh=fine, in_specs=in_specs, out_specs=(rows, rows), check_vma=False)
```

time: 595 us -> 187 us (0.31)
  waiting for transfers between devices: 417 us -> 41.7 us
  matrix products: 51.5 us -> 0 us
  starting transfers between devices: 12.1 us -> 60 us
  Pallas kernels: 0 us -> 44.7 us
  local copies, waits for them, and re-layouts: 43.5 us -> 5.69 us
  other arithmetic: 22 us -> 1.46 us
  between operations: 14.8 us -> 3.16 us
    psum x1 -> x0, waiting for transfers between devices: 231 us -> none  [broadcast(): return lax.psum(block, axis)]
    all_gather x3 -> x0, waiting for transfers between devices: 179 us -> none  [the longest x1 92.6 us: on_device(): full_text = lax.all_gather(owned_text, 'head', axis=3, tiled=True)]
    dot_general x4 -> x0, matrix products: 51.5 us -> none  [the longest x1 22.6 us: on_device(): jnp.einsum('htn,nhd->htd', weights.astype(jnp.bfloat16), value_rows, pref...]
    pallas_call x0 -> x11, Pallas kernels: none -> 44.7 us  [the longest x5 36.3 us: self_step(): call(functools.partial(self_kernel, len(shards), first, last), out_shape,...]
    all_to_all x2 -> x0, blocking collectives: 32 us -> none  [the longest x1 16.5 us: on_device(): lax.all_to_all(self_values, 'head', split_axis=1, concat_axis=0, tiled=True)]
    all_gather x0 -> x1, blocking collectives: none -> 29.1 us  [text_of_sample(): return lax.all_gather(piece, 'z', axis=0, tiled=True)]
    all_gather x2 -> x0, local copies, waits for them, and re-layouts: 28.6 us -> none  [the longest x1 14.3 us: on_device(): lax.all_gather(key_heads, 'seq', axis=0, tiled=True)]
    ppermute x0 -> x16, starting transfers between devices: none -> 24.6 us  [the longest x14 23 us: shift(): return lax.ppermute(block, 'z', [(z, (z + by) % size) for z in range(size)])]
  transfers between devices with their start and end apart: 6 -> 21, of which waited for: 6 -> 8; matrix products, arithmetic and copies ran while one was open for 13% -> 2% of each run, Pallas kernels for 0% -> 23%
where the time goes in v1:
time: 187 us; the launch traced here: 186 us
  starting transfers between devices  60 us (32%)
  Pallas kernels  44.7 us (24%)
  waiting for transfers between devices  41.7 us (22%)
  blocking collectives  29.1 us (16%)
  local copies, waits for them, and re-layouts  5.69 us (3%)
  between operations  3.16 us (2%)
    pallas_call x5, Pallas kernels, self_step(): call(functools.partial(self_kernel, len(shards), first, last), out_shape,...  36.3 us
    all_gather x1, blocking collectives, text_of_sample(): return lax.all_gather(piece, 'z', axis=0, tiled=True)  29.1 us
    all_to_all x4, starting transfers between devices, exchange(): lax.all_to_all(messages, PLANE, split_axis=0, concat_axis=0, tiled=True)  26.9 us
    ppermute x14, starting transfers between devices, shift(): return lax.ppermute(block, 'z', [(z, (z + by) % size) for z in range(size)])  23 us
    all_to_all x4, waiting for transfers between devices, exchange(): lax.all_to_all(messages, PLANE, split_axis=0, concat_axis=0, tiled=True)  19.6 us
    ppermute x14, waiting for transfers between devices, shift(): return lax.ppermute(block, 'z', [(z, (z + by) % size) for z in range(size)])  10.9 us
    all_to_all x1, waiting for transfers between devices, text_of_sample(): lax.all_to_all(held.reshape(8, 160, HD), 'z', split_axis=0, concat_axis=0...  9.19 us
    all_to_all x1, starting transfers between devices, text_of_sample(): lax.all_to_all(held.reshape(8, 160, HD), 'z', split_axis=0, concat_axis=0...  8.47 us
  transfers between devices with their start and end apart: 21, of which 8 were waited for; matrix products, arithmetic and copies ran while one was open for 2% of the time, Pallas kernels for 23%

profile of v1, /device:TPU:8, one launch (start us, length us, event | category | flops | bytes accessed | tf_op | source)
XLA Modules:
  0.0 185.9 jit_solution(834863476634675145)
XLA Ops:
  7.8 7.2 %all-to-all-start = ((bf16[32,80,128]{2,1,0:T(8,128)(2,1)}), bf16[32,80,128]{2,1,0:T(8,128)(2,1)S(1)}, u32[]{:S(2)}, u32[]{:S(2)}) async-start(bf16[32,80,128]{2,1,0:T(8,128)(2,1)} %shard_map.105), calls=%async_computation | async-start | bytes 1310720 | tf_op jit(solution)/shard_map/all_to_all | solution.py:276
  16.1 11.1 %all-to-all-done = bf16[32,80,128]{2,1,0:T(8,128)(2,1)S(1)} async-done(((bf16[32,80,128]{2,1,0:T(8,128)(2,1)}), bf16[32,80,128]{2,1,0:T(8,128)(2,1)S(1)}, u32[]{:S(2)}, u32[]{:S(2)}) %all-to-all-start) | async-done | bytes 655392 | tf_op jit(solution)/shard_map/all_to_all | solution.py:276
  27.1 8.5 %all-to-all-start.3 = ((bf16[8,160,128]{2,1,0:T(8,128)(2,1)}), bf16[8,160,128]{2,1,0:T(8,128)(2,1)S(1)}, u32[]{:S(2)}, u32[]{:S(2)}) async-start(bf16[8,160,128]{2,1,0:T(8,128)(2,1)} %bitcast.6), calls=%async_computation.3 | async-start | bytes 655360 | tf_op jit(solution)/shard_map/all_to_all | solution.py:300
  36.8 2.1 %collective-permute-start = (bf16[16,80,128]{2,1,0:T(8,128)(2,1)S(1)}, bf16[16,80,128]{2,1,0:T(8,128)(2,1)S(1)}, u32[]{:S(2)}, u32[]{:S(2)}) collective-permute-start(bf16[16,80,128]{2,1,0:T(8,128)(2,1)S(1)} %get-tuple-element.35.refs_1_), channel_id=1, source_target_pairs={{0,32},{32,64},{64,96},{96,128},{128,160},{160,192},{192,224},{224... | collective-permute-start | bytes 983048 | tf_op jit(solution)/shard_map/ppermute | solution.py:281
  40.2 9.2 %all-to-all-done.3 = bf16[8,160,128]{2,1,0:T(8,128)(2,1)S(1)} async-done(((bf16[8,160,128]{2,1,0:T(8,128)(2,1)}), bf16[8,160,128]{2,1,0:T(8,128)(2,1)S(1)}, u32[]{:S(2)}, u32[]{:S(2)}) %all-to-all-start.3) | async-done | bytes 327712 | tf_op jit(solution)/shard_map/all_to_all | solution.py:300
  50.1 4.8 %all-to-all-start.1 = ((bf16[32,128,128]{2,1,0:T(8,128)(2,1)}), bf16[32,128,128]{2,1,0:T(8,128)(2,1)S(1)}, u32[]{:S(2)}, u32[]{:S(2)}) async-start(bf16[32,128,128]{2,1,0:T(8,128)(2,1)} %shard_map.104), calls=%async_computation.1 | async-start | bytes 2097152 | tf_op jit(solution)/shard_map/all_to_all | solution.py:276
  55.9 2.3 %collective-permute-start.11 = (bf16[16,80,128]{2,1,0:T(8,128)(2,1)S(1)}, bf16[16,80,128]{2,1,0:T(8,128)(2,1)}, u32[]{:S(2)}, u32[]{:S(2)}) collective-permute-start(bf16[16,80,128]{2,1,0:T(8,128)(2,1)S(1)} %get-tuple-element.35.refs_1_), channel_id=1, source_target_pairs={{0,224},{32,0},{64,32},{96,64},{128,96},{160,128},{192,160},{224,1... | collective-permute-start | bytes 983048 | tf_op jit(solution)/shard_map/ppermute | solution.py:281
  59.0 3.2 %collective-permute-start.5 = (bf16[16,80,128]{2,1,0:T(8,128)(2,1)S(1)}, bf16[16,80,128]{2,1,0:T(8,128)(2,1)}, u32[]{:S(2)}, u32[]{:S(2)}) collective-permute-start(bf16[16,80,128]{2,1,0:T(8,128)(2,1)S(1)} %collective-permute-done.4.refs_4_), channel_id=1, source_target_pairs={{0,224},{32,0},{64,32},{96,64},{128,96},{160,128},{192,160},{224,1... | collective-permute-start | bytes 983048 | tf_op jit(solution)/shard_map/ppermute | solution.py:281
  62.2 4.7 %collective-permute-done.8.refs_2_ = bf16[16,80,128]{2,1,0:T(8,128)(2,1)} collective-permute-done((bf16[16,80,128]{2,1,0:T(8,128)(2,1)S(1)}, bf16[16,80,128]{2,1,0:T(8,128)(2,1)}, u32[]{:S(2)}, u32[]{:S(2)}) %collective-permute-start.8) | collective-permute-done | bytes 327712 | tf_op jit(solution)/shard_map/ppermute | solution.py:281
  66.9 3.3 %collective-permute-start.12 = (bf16[16,80,128]{2,1,0:T(8,128)(2,1)}, bf16[16,80,128]{2,1,0:T(8,128)(2,1)}, u32[]{:S(2)}, u32[]{:S(2)}) collective-permute-start(bf16[16,80,128]{2,1,0:T(8,128)(2,1)} %collective-permute-done.11.refs_3_), channel_id=1, source_target_pairs={{0,224},{32,0},{64,32},{96,64},{128,96},{160,128},{192,160},{224,1... | collective-permute-start | bytes 983048 | tf_op jit(solution)/shard_map/ppermute | solution.py:281
  70.9 3.1 %collective-permute-done.1.refs_1_ = bf16[16,80,128]{2,1,0:T(8,128)(2,1)} collective-permute-done((bf16[16,80,128]{2,1,0:T(8,128)(2,1)S(1)}, bf16[16,80,128]{2,1,0:T(8,128)(2,1)}, u32[]{:S(2)}, u32[]{:S(2)}) %collective-permute-start.1) | collective-permute-done | bytes 327712 | tf_op jit(solution)/shard_map/ppermute | solution.py:281
  73.9 3.3 %collective-permute-start.6 = (bf16[16,80,128]{2,1,0:T(8,128)(2,1)}, bf16[16,80,128]{2,1,0:T(8,128)(2,1)}, u32[]{:S(2)}, u32[]{:S(2)}) collective-permute-start(bf16[16,80,128]{2,1,0:T(8,128)(2,1)} %collective-permute-done.5.refs_4_), channel_id=1, source_target_pairs={{0,224},{32,0},{64,32},{96,64},{128,96},{160,128},{192,160},{224,1... | collective-permute-start | bytes 983048 | tf_op jit(solution)/shard_map/ppermute | solution.py:281
  77.8 3.1 %collective-permute-done.9.refs_2_ = bf16[16,80,128]{2,1,0:T(8,128)(2,1)} collective-permute-done((bf16[16,80,128]{2,1,0:T(8,128)(2,1)}, bf16[16,80,128]{2,1,0:T(8,128)(2,1)}, u32[]{:S(2)}, u32[]{:S(2)}) %collective-permute-start.9) | collective-permute-done | bytes 327712 | tf_op jit(solution)/shard_map/ppermute | solution.py:281
  80.9 3.3 %collective-permute-start.13 = (bf16[16,80,128]{2,1,0:T(8,128)(2,1)}, bf16[16,80,128]{2,1,0:T(8,128)(2,1)}, u32[]{:S(2)}, u32[]{:S(2)}) collective-permute-start(bf16[16,80,128]{2,1,0:T(8,128)(2,1)} %collective-permute-done.12.refs_3_), channel_id=1, source_target_pairs={{0,224},{32,0},{64,32},{96,64},{128,96},{160,128},{192,160},{224,1... | collective-permute-start | bytes 983048 | tf_op jit(solution)/shard_map/ppermute | solution.py:281
  85.0 29.1 %all-gather = bf16[1,1280,128]{2,1,0:T(8,128)(2,1)S(1)} all-gather(bf16[1,160,128]{2,1,0:T(8,128)(2,1)S(1)} %constant_dynamic-slice_fusion), channel_id=2, replica_groups=mesh['z'=8,'xl'=2,'core'=2,'xh'=2,'y'=4] {'z'}, dimensions={1}, use_global_device_ids=true | all-gather | bytes 368640 | tf_op jit(solution)/shard_map/all_gather | solution.py:302
  117.4 4.1 %shard_map.113 = bf16[32,80,128]{2,1,0:T(8,128)(2,1)} custom-call(s32[2]{0:T(128)S(1)} %pad_add_fusion.scalars_ref, bf16[32,128,128]{2,1,0:T(8,128)(2,1)S(1)} %all-to-all-done.1.refs_0_.queries_ref, bf16[1280,128]{1,0:T(8,128)(2,1)S(1)} %bitcast.11), custom_call_target="tpu_custom_call" | custom-call | flops 671088640 | bytes 2097152 | tf_op jit(solution)/shard_map/pallas_call | solution.py:225
  121.5 7.4 %all-to-all-start.4 = ((bf16[32,80,128]{2,1,0:T(8,128)(2,1)}), bf16[32,80,128]{2,1,0:T(8,128)(2,1)S(1)}, u32[]{:S(2)}, u32[]{:S(2)}) async-start(bf16[32,80,128]{2,1,0:T(8,128)(2,1)} %shard_map.113), calls=%async_computation.4 | async-start | bytes 1310720 | tf_op jit(solution)/shard_map/all_to_all | solution.py:276
  128.9 3.7 %shard_map.106 = (f32[1024,128]{1,0:T(8,128)S(1)}, f32[1024,128]{1,0:T(8,128)S(1)}, f32[1024,128]{1,0:T(8,128)S(1)}) custom-call(bf16[32,128,128]{2,1,0:T(8,128)(2,1)S(1)} %all-to-all-done.1.refs_0_.queries_ref, bf16[16,80,128]{2,1,0:T(8,128)(2,1)S(1)} %get-tuple-element.35.refs_1_, bf16[16,80,128]{2,1,0:T(8,128)(2,1)S(1)} %get-tuple-element.34.refs_2_), custom_call_target="tpu_custom_call" | custom-call | flops 1342177280 | bytes 2752512 | tf_op jit(solution)/shard_map/pallas_call | solution.py:191
  132.6 8.3 %shard_map.107 = (f32[1024,128]{1,0:T(8,128)S(1)}, f32[1024,128]{1,0:T(8,128)S(1)}, f32[1024,128]{1,0:T(8,128)S(1)}) custom-call(bf16[32,128,128]{2,1,0:T(8,128)(2,1)S(1)} %all-to-all-done.1.refs_0_.queries_ref, bf16[16,80,128]{2,1,0:T(8,128)(2,1)S(1)} %copy-done.7, bf16[16,80,128]{2,1,0:T(8,128)(2,1)} %collective-permute-done.8.refs_2_, ...), custom_call_target="tpu_custom_call" | custom-call | flops 2684354560 | bytes 3407872 | tf_op jit(solution)/shard_map/pallas_call | solution.py:191
  140.9 8.5 %shard_map.108 = (f32[1024,128]{1,0:T(8,128)S(1)}, f32[1024,128]{1,0:T(8,128)S(1)}, f32[1024,128]{1,0:T(8,128)S(1)}) custom-call(bf16[32,128,128]{2,1,0:T(8,128)(2,1)S(1)} %all-to-all-done.1.refs_0_.queries_ref, bf16[16,80,128]{2,1,0:T(8,128)(2,1)} %collective-permute-done.1.refs_1_, bf16[16,80,128]{2,1,0:T(8,128)(2,1)} %collective-permute-done.9.refs_2_, ...), custom_call_target="tpu_custom_call" | custom-call | flops 2684354560 | bytes 3407872 | tf_op jit(solution)/shard_map/pallas_call | solution.py:191
  149.4 8.5 %shard_map.109 = (f32[1024,128]{1,0:T(8,128)S(1)}, f32[1024,128]{1,0:T(8,128)S(1)}, f32[1024,128]{1,0:T(8,128)S(1)}) custom-call(bf16[32,128,128]{2,1,0:T(8,128)(2,1)S(1)} %all-to-all-done.1.refs_0_.queries_ref, bf16[16,80,128]{2,1,0:T(8,128)(2,1)} %collective-permute-done.2.refs_1_, bf16[16,80,128]{2,1,0:T(8,128)(2,1)} %collective-permute-done.10.refs_2_, ...), custom_call_target="tpu_custom_call" | custom-call | flops 2684354560 | bytes 3407872 | tf_op jit(solution)/shard_map/pallas_call | solution.py:191
  158.0 7.2 %shard_map.110 = bf16[32,80,128]{2,1,0:T(8,128)(2,1)} custom-call(bf16[32,128,128]{2,1,0:T(8,128)(2,1)S(1)} %all-to-all-done.1.refs_0_.queries_ref, bf16[16,80,128]{2,1,0:T(8,128)(2,1)} %collective-permute-done.3.refs_1_, bf16[16,80,128]{2,1,0:T(8,128)(2,1)} %collective-permute-done.7.refs_2_, f32[1024,128]{1,0:T(8,128)S(1)} %get-tuple-element.29.refs_3_, ...), custom_call_target="tpu_custom_call" | custom-call | flops 1342177280 | bytes 2752512 | tf_op jit(solution)/shard_map/pallas_call | solution.py:191
  165.2 7.5 %all-to-all-start.2 = ((bf16[32,80,128]{2,1,0:T(8,128)(2,1)}), bf16[32,80,128]{2,1,0:T(8,128)(2,1)S(1)}, u32[]{:S(2)}, u32[]{:S(2)}) async-start(bf16[32,80,128]{2,1,0:T(8,128)(2,1)} %shard_map.110), calls=%async_computation.2 | async-start | bytes 1310720 | tf_op jit(solution)/shard_map/all_to_all | solution.py:276
  176.3 8.5 %all-to-all-done.2.refs_0_ = bf16[32,80,128]{2,1,0:T(8,128)(2,1)S(1)} async-done(((bf16[32,80,128]{2,1,0:T(8,128)(2,1)}), bf16[32,80,128]{2,1,0:T(8,128)(2,1)S(1)}, u32[]{:S(2)}, u32[]{:S(2)}) %all-to-all-start.2) | async-done | bytes 655392 | tf_op jit(solution)/shard_map/all_to_all | solution.py:276
  (67 shorter events, 20.8 us)
Async XLA Ops:
  0.6 174.7 %copy-start = (f32[50,5120]{1,0:T(8,128)S(1)}, f32[50,5120]{1,0:T(8,128)}, u32[]{:S(2)}) copy-start(f32[50,5120]{1,0:T(8,128)} %param.17) | copy-start | bytes 3072004
  2.3 2.2 %collective-permute-start.14 = (bf16[2,1280,128]{2,1,0:T(8,128)(2,1)S(1)}, bf16[2,1280,128]{2,1,0:T(8,128)(2,1)S(1)}, u32[]{:S(2)}, u32[]{:S(2)}) collective-permute-start(bf16[2,1280,128]{2,1,0:T(8,128)(2,1)S(1)} %get-tuple-element.33), channel_id=1, source_target_pairs={{0,8},{8,0},{1,9},{9,1},{2,10},{10,2},{3,11},{11,3},{4,12},{12,4},... | collective-permute-start | bytes 1966088 | tf_op jit(solution)/shard_map/ppermute | solution.py:296
  5.3 10.0 %collective-permute-start.15 = (bf16[1280,128]{1,0:T(8,128)(2,1)}, bf16[1280,128]{1,0:T(8,128)(2,1)S(1)}, u32[]{:S(2)}, u32[]{:S(2)}) collective-permute-start(bf16[1280,128]{1,0:T(8,128)(2,1)} %dynamic-slice_bitcast_fusion), channel_id=1, source_target_pairs={{0,16},{16,0},{1,17},{17,1},{2,18},{18,2},{3,19},{19,3},{4,20},{20... | collective-permute-start | bytes 983048 | tf_op jit(solution)/shard_map/ppermute | solution.py:298
  7.8 19.3 %all-to-all-start = ((bf16[32,80,128]{2,1,0:T(8,128)(2,1)}), bf16[32,80,128]{2,1,0:T(8,128)(2,1)S(1)}, u32[]{:S(2)}, u32[]{:S(2)}) async-start(bf16[32,80,128]{2,1,0:T(8,128)(2,1)} %shard_map.105), calls=%async_computation | async-start | bytes 1310720 | tf_op jit(solution)/shard_map/all_to_all | solution.py:276
  27.1 22.3 %all-to-all-start.3 = ((bf16[8,160,128]{2,1,0:T(8,128)(2,1)}), bf16[8,160,128]{2,1,0:T(8,128)(2,1)S(1)}, u32[]{:S(2)}, u32[]{:S(2)}) async-start(bf16[8,160,128]{2,1,0:T(8,128)(2,1)} %bitcast.6), calls=%async_computation.3 | async-start | bytes 655360 | tf_op jit(solution)/shard_map/all_to_all | solution.py:300
  36.8 33.5 %copy-start.12 = (s32[32]{0:T(128)S(1)}, s32[32]{0:T(128)}, u32[]{:S(2)}) copy-start(s32[32]{0:T(128)} %param.15) | copy-start | bytes 388
  36.8 21.5 %collective-permute-start = (bf16[16,80,128]{2,1,0:T(8,128)(2,1)S(1)}, bf16[16,80,128]{2,1,0:T(8,128)(2,1)S(1)}, u32[]{:S(2)}, u32[]{:S(2)}) collective-permute-start(bf16[16,80,128]{2,1,0:T(8,128)(2,1)S(1)} %get-tuple-element.35.refs_1_), channel_id=1, source_target_pairs={{0,32},{32,64},{64,96},{96,128},{128,160},{160,192},{192,224},{224... | collective-permute-start | bytes 983048 | tf_op jit(solution)/shard_map/ppermute | solution.py:281
  38.9 20.1 %collective-permute-start.4 = (bf16[16,80,128]{2,1,0:T(8,128)(2,1)S(1)}, bf16[16,80,128]{2,1,0:T(8,128)(2,1)S(1)}, u32[]{:S(2)}, u32[]{:S(2)}) collective-permute-start(bf16[16,80,128]{2,1,0:T(8,128)(2,1)S(1)} %get-tuple-element.34.refs_2_), channel_id=1, source_target_pairs={{0,224},{32,0},{64,32},{96,64},{128,96},{160,128},{192,160},{224,1... | collective-permute-start | bytes 983048 | tf_op jit(solution)/shard_map/ppermute | solution.py:281
  50.1 67.3 %all-to-all-start.1 = ((bf16[32,128,128]{2,1,0:T(8,128)(2,1)}), bf16[32,128,128]{2,1,0:T(8,128)(2,1)S(1)}, u32[]{:S(2)}, u32[]{:S(2)}) async-start(bf16[32,128,128]{2,1,0:T(8,128)(2,1)} %shard_map.104), calls=%async_computation.1 | async-start | bytes 2097152 | tf_op jit(solution)/shard_map/all_to_all | solution.py:276
  54.9 11.9 %collective-permute-start.8 = (bf16[16,80,128]{2,1,0:T(8,128)(2,1)S(1)}, bf16[16,80,128]{2,1,0:T(8,128)(2,1)}, u32[]{:S(2)}, u32[]{:S(2)}) collective-permute-start(bf16[16,80,128]{2,1,0:T(8,128)(2,1)S(1)} %get-tuple-element.34.refs_2_), channel_id=1, source_target_pairs={{0,32},{32,64},{64,96},{96,128},{128,160},{160,192},{192,224},{224... | collective-permute-start | bytes 983048 | tf_op jit(solution)/shard_map/ppermute | solution.py:281
  55.9 11.0 %collective-permute-start.11 = (bf16[16,80,128]{2,1,0:T(8,128)(2,1)S(1)}, bf16[16,80,128]{2,1,0:T(8,128)(2,1)}, u32[]{:S(2)}, u32[]{:S(2)}) collective-permute-start(bf16[16,80,128]{2,1,0:T(8,128)(2,1)S(1)} %get-tuple-element.35.refs_1_), channel_id=1, source_target_pairs={{0,224},{32,0},{64,32},{96,64},{128,96},{160,128},{192,160},{224,1... | collective-permute-start | bytes 983048 | tf_op jit(solution)/shard_map/ppermute | solution.py:281
  58.3 15.7 %collective-permute-start.1 = (bf16[16,80,128]{2,1,0:T(8,128)(2,1)S(1)}, bf16[16,80,128]{2,1,0:T(8,128)(2,1)}, u32[]{:S(2)}, u32[]{:S(2)}) collective-permute-start(bf16[16,80,128]{2,1,0:T(8,128)(2,1)S(1)} %collective-permute-done.refs_1_), channel_id=1, source_target_pairs={{0,32},{32,64},{64,96},{96,128},{128,160},{160,192},{192,224},{224... | collective-permute-start | bytes 983048 | tf_op jit(solution)/shard_map/ppermute | solution.py:281
  59.0 62.5 %copy-start.8 = (bf16[16,80,128]{2,1,0:T(8,128)(2,1)}, bf16[16,80,128]{2,1,0:T(8,128)(2,1)S(1)}, u32[]{:S(2)}) copy-start(bf16[16,80,128]{2,1,0:T(8,128)(2,1)S(1)} %collective-permute-done.4.refs_4_) | copy-start | bytes 983044
  59.0 14.9 %collective-permute-start.5 = (bf16[16,80,128]{2,1,0:T(8,128)(2,1)S(1)}, bf16[16,80,128]{2,1,0:T(8,128)(2,1)}, u32[]{:S(2)}, u32[]{:S(2)}) collective-permute-start(bf16[16,80,128]{2,1,0:T(8,128)(2,1)S(1)} %collective-permute-done.4.refs_4_), channel_id=1, source_target_pairs={{0,224},{32,0},{64,32},{96,64},{128,96},{160,128},{192,160},{224,1... | collective-permute-start | bytes 983048 | tf_op jit(solution)/shard_map/ppermute | solution.py:281
  66.9 14.0 %collective-permute-start.9 = (bf16[16,80,128]{2,1,0:T(8,128)(2,1)}, bf16[16,80,128]{2,1,0:T(8,128)(2,1)}, u32[]{:S(2)}, u32[]{:S(2)}) collective-permute-start(bf16[16,80,128]{2,1,0:T(8,128)(2,1)} %collective-permute-done.8.refs_2_), channel_id=1, source_target_pairs={{0,32},{32,64},{64,96},{96,128},{128,160},{160,192},{192,224},{224... | collective-permute-start | bytes 983048 | tf_op jit(solution)/shard_map/ppermute | solution.py:281
  66.9 14.0 %collective-permute-start.12 = (bf16[16,80,128]{2,1,0:T(8,128)(2,1)}, bf16[16,80,128]{2,1,0:T(8,128)(2,1)}, u32[]{:S(2)}, u32[]{:S(2)}) collective-permute-start(bf16[16,80,128]{2,1,0:T(8,128)(2,1)} %collective-permute-done.11.refs_3_), channel_id=1, source_target_pairs={{0,224},{32,0},{64,32},{96,64},{128,96},{160,128},{192,160},{224,1... | collective-permute-start | bytes 983048 | tf_op jit(solution)/shard_map/ppermute | solution.py:281
  73.9 40.2 %collective-permute-start.2 = (bf16[16,80,128]{2,1,0:T(8,128)(2,1)}, bf16[16,80,128]{2,1,0:T(8,128)(2,1)}, u32[]{:S(2)}, u32[]{:S(2)}) collective-permute-start(bf16[16,80,128]{2,1,0:T(8,128)(2,1)} %collective-permute-done.1.refs_1_), channel_id=1, source_target_pairs={{0,32},{32,64},{64,96},{96,128},{128,160},{160,192},{192,224},{224... | collective-permute-start | bytes 983048 | tf_op jit(solution)/shard_map/ppermute | solution.py:281
  73.9 42.0 %collective-permute-start.6 = (bf16[16,80,128]{2,1,0:T(8,128)(2,1)}, bf16[16,80,128]{2,1,0:T(8,128)(2,1)}, u32[]{:S(2)}, u32[]{:S(2)}) collective-permute-start(bf16[16,80,128]{2,1,0:T(8,128)(2,1)} %collective-permute-done.5.refs_4_), channel_id=1, source_target_pairs={{0,224},{32,0},{64,32},{96,64},{128,96},{160,128},{192,160},{224,1... | collective-permute-start | bytes 983048 | tf_op jit(solution)/shard_map/ppermute | solution.py:281
  80.9 68.5 %collective-permute-start.10 = (bf16[16,80,128]{2,1,0:T(8,128)(2,1)}, bf16[16,80,128]{2,1,0:T(8,128)(2,1)}, u32[]{:S(2)}, u32[]{:S(2)}) collective-permute-start(bf16[16,80,128]{2,1,0:T(8,128)(2,1)} %collective-permute-done.9.refs_2_), channel_id=1, source_target_pairs={{0,32},{32,64},{64,96},{96,128},{128,160},{160,192},{192,224},{224... | collective-permute-start | bytes 983048 | tf_op jit(solution)/shard_map/ppermute | solution.py:281
  80.9 68.5 %collective-permute-start.13 = (bf16[16,80,128]{2,1,0:T(8,128)(2,1)}, bf16[16,80,128]{2,1,0:T(8,128)(2,1)}, u32[]{:S(2)}, u32[]{:S(2)}) collective-permute-start(bf16[16,80,128]{2,1,0:T(8,128)(2,1)} %collective-permute-done.12.refs_3_), channel_id=1, source_target_pairs={{0,224},{32,0},{64,32},{96,64},{128,96},{160,128},{192,160},{224,1... | collective-permute-start | bytes 983048 | tf_op jit(solution)/shard_map/ppermute | solution.py:281
  114.1 43.9 %collective-permute-start.3 = (bf16[16,80,128]{2,1,0:T(8,128)(2,1)}, bf16[16,80,128]{2,1,0:T(8,128)(2,1)}, u32[]{:S(2)}, u32[]{:S(2)}) collective-permute-start(bf16[16,80,128]{2,1,0:T(8,128)(2,1)} %collective-permute-done.2.refs_1_), channel_id=1, source_target_pairs={{0,32},{32,64},{64,96},{96,128},{128,160},{160,192},{192,224},{224... | collective-permute-start | bytes 983048 | tf_op jit(solution)/shard_map/ppermute | solution.py:281
  115.9 42.1 %collective-permute-start.7 = (bf16[16,80,128]{2,1,0:T(8,128)(2,1)}, bf16[16,80,128]{2,1,0:T(8,128)(2,1)}, u32[]{:S(2)}, u32[]{:S(2)}) collective-permute-start(bf16[16,80,128]{2,1,0:T(8,128)(2,1)} %collective-permute-done.6.refs_4_), channel_id=1, source_target_pairs={{0,224},{32,0},{64,32},{96,64},{128,96},{160,128},{192,160},{224,1... | collective-permute-start | bytes 983048 | tf_op jit(solution)/shard_map/ppermute | solution.py:281
  121.5 43.8 %all-to-all-start.4 = ((bf16[32,80,128]{2,1,0:T(8,128)(2,1)}), bf16[32,80,128]{2,1,0:T(8,128)(2,1)S(1)}, u32[]{:S(2)}, u32[]{:S(2)}) async-start(bf16[32,80,128]{2,1,0:T(8,128)(2,1)} %shard_map.113), calls=%async_computation.4 | async-start | bytes 1310720 | tf_op jit(solution)/shard_map/all_to_all | solution.py:276
  165.2 19.6 %all-to-all-start.2 = ((bf16[32,80,128]{2,1,0:T(8,128)(2,1)}), bf16[32,80,128]{2,1,0:T(8,128)(2,1)S(1)}, u32[]{:S(2)}, u32[]{:S(2)}) async-start(bf16[32,80,128]{2,1,0:T(8,128)(2,1)} %shard_map.110), calls=%async_computation.2 | async-start | bytes 1310720 | tf_op jit(solution)/shard_map/all_to_all | solution.py:276
  (11 other events, 65.3 us)

commit v2 on v1

v2 whole, which is shorter than its diff:
```python
import functools
import math

import jax
import jax.numpy as jnp
from jax import lax
from jax.experimental import pallas as pl
from jax.experimental.pallas import tpu as pltpu
from jax.sharding import Mesh, PartitionSpec as P

AXES = ("z", "xl", "core", "xh", "y")
SIZES = (8, 2, 2, 2, 4)
PLANES = SIZES[0]
PLANE = ("xl", "core", "xh", "y")
COLUMN = ("z", "y")
RING = ("xl", "xh")
RING_ORDER = (0, 2, 1, 3)

HD = 128
ROWS = 32
GROUPS = 8
SPLIT = 4
PEERS = GROUPS * SPLIT
PLANE_ROWS = PEERS * ROWS
TEXT = 512
SCALE = math.log2(math.e) / math.sqrt(HD)
F32 = jnp.float32
BF16 = jnp.bfloat16
VMEM_LIMIT = 62 * 1024 * 1024


def whole_block(shape):
    return pl.BlockSpec(shape, lambda step: (0,) * len(shape))


def call(kernel, out_shape, operands, cost=None, scalars=0, specs=()):
    in_specs = [pl.BlockSpec(memory_space=pltpu.SMEM)] * scalars + list(specs)
    in_specs += [whole_block(x.shape) for x in operands[len(in_specs) :]]
    return pl.pallas_call(
        kernel,
        out_shape=out_shape,
        grid=(1,),
        in_specs=in_specs,
        out_specs=jax.tree.map(lambda x: whole_block(x.shape), out_shape),
        cost_estimate=cost,
        compiler_params=pltpu.CompilerParams(vmem_limit_bytes=VMEM_LIMIT),
    )(*operands)


def query_rows():
    return pl.BlockSpec((PEERS, 64, HD), lambda step: (0, 0, 0))


def head_columns(head):
    return slice(head * HD, (head + 1) * HD)


def self_slot(i, j):
    return j * SPLIT + i


def cross_slot(i, j):
    return i * GROUPS + j


def pack_kernel(keys_ref, values_ref, queries_ref, out_ref):
    quarter = ROWS // SPLIT
    for j in range(GROUPS):
        fifth = head_columns(5 * j + 4)
        key_rows = keys_ref[:, fifth].astype(F32)
        value_rows = values_ref[:, fifth].astype(F32)
        for i in range(SPLIT):
            to = self_slot(i, j)
            own = head_columns(5 * j + i)
            out_ref[to, 0:32, :] = queries_ref[:, own]
            out_ref[to, 32:64, :] = queries_ref[:, fifth]
            out_ref[to, 64:96, :] = keys_ref[:, own]
            out_ref[to, 96:128, :] = values_ref[:, own]
            part = slice(i * quarter, (i + 1) * quarter)
            out_ref[to, 128:144, :] = jnp.concatenate([key_rows[part], value_rows[part]]).astype(BF16)


def pack_queries_kernel(queries_ref, out_ref):
    for j in range(GROUPS):
        for i in range(SPLIT):
            to = cross_slot(i, j)
            out_ref[to, 0:32, :] = queries_ref[:, head_columns(5 * j + i)]
            out_ref[to, 32:64, :] = queries_ref[:, head_columns(5 * j + 4)]


def pack_text_kernel(core_ref, text_ref, keep_ref, send_ref):
    quarter = TEXT // SPLIT

    def write(ref, core):
        for xl in range(2):
            i = xl * 2 + core
            for kind in range(2):
                base = kind * (TEXT + quarter)
                ref[xl, base : base + TEXT, :] = text_ref[0, kind, :, head_columns(i)]
                ref[xl, base + TEXT : base + TEXT + quarter, :] = text_ref[
                    0, kind, i * quarter : (i + 1) * quarter, head_columns(4)
                ]

    @pl.when(core_ref[0] == 0)
    def _():
        write(keep_ref, 0)
        write(send_ref, 1)

    @pl.when(core_ref[0] != 0)
    def _():
        write(keep_ref, 1)
        write(send_ref, 0)


def scaled_queries(queries):
    scaled = queries.astype(F32) * SCALE
    high = scaled.astype(BF16)
    low = (scaled - high.astype(F32)).astype(BF16)
    return jnp.concatenate([high, low], axis=1)


def products(queries, keys):
    return lax.dot_general(queries, keys, (((1,), (1,)), ((), ())), preferred_element_type=F32)


def twice(keys):
    return jnp.concatenate([keys, keys], axis=1)


def with_ones(values):
    return jnp.concatenate([values, jnp.ones_like(values)], axis=1)


def fold(scores, values, state):
    top = jnp.max(scores, axis=1, keepdims=True)
    if state is not None:
        top = jnp.maximum(top, state[0])
    weights = jnp.exp2(scores - top).astype(BF16)
    summed = jnp.dot(weights, values, preferred_element_type=F32)
    total, summed = summed[:, HD : HD + 1], summed[:, :HD]
    if state is not None:
        shrink = jnp.exp2(state[0] - top)
        total = total + state[1] * shrink
        summed = summed + state[2] * shrink
    return top, total, summed


def write_result(out_ref, to, whole, part):
    count = to.size
    out_ref[to, 0:32, :] = (whole[2] / whole[1]).astype(BF16).reshape(count, ROWS, HD)
    out_ref[to, 32:64, :] = (part[2] / part[1]).astype(BF16).reshape(count, ROWS, HD)
    size = part[0] + jnp.log2(part[1])
    size = jnp.broadcast_to(size, (count * ROWS, HD))
    high = size.astype(BF16).astype(F32)
    middle = (size - high).astype(BF16).astype(F32)
    low = size - high - middle
    lane = lax.broadcasted_iota(jnp.int32, (count * ROWS, HD), 1)
    row = lax.broadcasted_iota(jnp.int32, (count * ROWS, HD), 0)
    terms = jnp.where(lane < 32, high, jnp.where(lane < 64, middle, low))
    terms = jnp.where((lane % 32 == row % 32) & (lane < 96), terms, 0.0)
    terms = jnp.sum(terms.reshape(count, ROWS, HD), axis=1, keepdims=True)
    out_ref[to, 64:80, :] = jnp.broadcast_to(terms, (count, 16, HD)).astype(BF16)


def fold_lazily(scaled, keys, values, state):
    top, total, summed = state
    excess = None
    for at in range(0, keys.shape[0], CHUNK):
        part = slice(at, min(at + CHUNK, keys.shape[0]))
        scores = products(scaled, keys[part]) - top
        most = jnp.max(scores.reshape(-1, 8, scores.shape[1]), axis=0)
        most = functools.reduce(jnp.maximum, [most[:, t : t + HD] for t in range(0, most.shape[1], HD)])
        excess = most if excess is None else jnp.maximum(excess, most)
        term = jnp.dot(jnp.exp2(scores).astype(BF16), values[part], preferred_element_type=F32)
        total = total + term[:, HD : HD + 1]
        summed = summed + term[:, :HD]
    return (top, total, summed), excess


SENDERS = 8
CHUNK = 512
MOST = 64.0


def keys_and_values(shard_refs):
    keys, values, part_keys, part_values = [], [], [], []
    for ref in shard_refs:
        count = ref.shape[0]
        keys.append(ref[:, 0:32, :].reshape(count * 32, HD))
        values.append(ref[:, 32:64, :].reshape(count * 32, HD))
        quarter = ref[:, 64:80, :].astype(F32)
        part_keys.append(quarter[:, 0:8].reshape(count * 8, HD).astype(BF16))
        part_values.append(quarter[:, 8:16].reshape(count * 8, HD).astype(BF16))
    return (
        (twice(jnp.concatenate(keys)), with_ones(jnp.concatenate(values))),
        (twice(jnp.concatenate(part_keys)), with_ones(jnp.concatenate(part_values))),
    )


def self_kernel(shards, first, last, *refs):
    queries_ref, shard_refs, rest = refs[0], refs[1 : 1 + shards], refs[1 + shards :]
    if not first:
        whole_ref, part_ref, stats_ref = rest[:3]
        rest = rest[3:]
    block = SENDERS * ROWS

    def queries_of(senders):
        return [scaled_queries(queries_ref[senders, at : at + 32, :].reshape(block, HD)) for at in (0, 32)]

    def states_of(rows):
        stats = stats_ref[rows]
        return (stats[:, 0:1], stats[:, 1:2], whole_ref[rows]), (stats[:, 2:3], stats[:, 3:4], part_ref[rows])

    def write(senders, rows, whole, part):
        if last:
            write_result(rest[0], senders, whole, part)
            return
        whole_out, part_out, stats_out = rest
        whole_out[rows] = whole[2]
        part_out[rows] = part[2]
        lane = lax.broadcasted_iota(jnp.int32, (block, HD), 1)
        stats_out[rows] = jnp.where(
            lane == 0, whole[0], jnp.where(lane == 1, whole[1], jnp.where(lane == 2, part[0], part[1]))
        )

    def places(index):
        start = index * block if isinstance(index, int) else pl.multiple_of(index * block, block)
        return pl.ds(index * SENDERS, SENDERS), pl.ds(start, block)

    pairs = keys_and_values(shard_refs)
    excess = None
    for index in range(PEERS // SENDERS):
        senders, rows = places(index)
        scaled = queries_of(senders)
        if first:
            write(senders, rows, *(fold(products(q, k), v, None) for q, (k, v) in zip(scaled, pairs)))
            continue
        done = [fold_lazily(q, k, v, state) for q, (k, v), state in zip(scaled, pairs, states_of(rows))]
        write(senders, rows, done[0][0], done[1][0])
        for _, most in done:
            excess = most if excess is None else jnp.maximum(excess, most)
    if first:
        return

    @pl.when(jnp.max(excess) > MOST)
    def _():
        again = keys_and_values(shard_refs)

        def redo(index, carry):
            senders, rows = places(index)
            found = [
                fold(products(q, k), v, state)
                for q, (k, v), state in zip(queries_of(senders), again, states_of(rows))
            ]
            write(senders, rows, *found)
            return carry

        lax.fori_loop(0, PEERS // SENDERS, redo, 0)


def self_step(queries, shards, state, last=False):
    first = state is None
    if last:
        out_shape = jax.ShapeDtypeStruct((PEERS, 80, HD), BF16)
    else:
        out_shape = [jax.ShapeDtypeStruct((PLANE_ROWS, HD), F32)] * 3
    keys = sum(s.shape[0] for s in shards) * 40
    cost = pl.CostEstimate(
        flops=4 * PLANE_ROWS * keys * HD * 2,
        bytes_accessed=keys * HD * 4 + PLANE_ROWS * HD * 16,
        transcendentals=PLANE_ROWS * keys,
    )
    operands = (queries, *shards, *(() if first else state))
    kernel = functools.partial(self_kernel, len(shards), first, last)
    return call(kernel, out_shape, operands, cost, specs=[query_rows()])


def cross_kernel(scalars_ref, queries_ref, text_ref, out_ref):
    length, place = scalars_ref[0], scalars_ref[1]
    quarter = TEXT // SPLIT
    block = SENDERS * ROWS

    def masked(scores, start):
        at = start + lax.broadcasted_iota(jnp.int32, scores.shape, 1)
        return jnp.where(at < length, scores, -1e30)

    keys, part_keys = twice(text_ref[0:512, :]), twice(text_ref[512:640, :])
    values, part_values = with_ones(text_ref[640:1152, :]), with_ones(text_ref[1152:1280, :])
    for index in range(PEERS // SENDERS):
        senders = pl.ds(index * SENDERS, SENDERS)
        scaled = [scaled_queries(queries_ref[senders, at : at + 32, :].reshape(block, HD)) for at in (0, 32)]
        whole = fold(masked(products(scaled[0], keys), 0), values, None)
        part = fold(masked(products(scaled[1], part_keys), place * quarter), part_values, None)
        write_result(out_ref, senders, whole, part)


def cross_step(scalars, queries, text):
    cost = pl.CostEstimate(
        flops=4 * PLANE_ROWS * 640 * HD * 2, bytes_accessed=2 * 1024 * 1024, transcendentals=PLANE_ROWS * 640
    )
    out_shape = jax.ShapeDtypeStruct((PEERS, 80, HD), BF16)
    return call(cross_kernel, out_shape, (scalars, queries, text), cost, scalars=1, specs=[query_rows()])


def merged(message_ref, slot, j):
    lane = lax.broadcasted_iota(jnp.int32, (ROWS, HD), 1)
    row = lax.broadcasted_iota(jnp.int32, (ROWS, HD), 0)
    mine = (lane % 32 == row) & (lane < 96)
    sizes = []
    for i in range(SPLIT):
        terms = message_ref[slot(i, j), 64:80, :].astype(F32)[0:1]
        sizes.append(jnp.sum(jnp.where(mine, jnp.broadcast_to(terms, (ROWS, HD)), 0.0), axis=1, keepdims=True))
    top = functools.reduce(jnp.maximum, sizes)
    shares = [jnp.exp2(s - top) for s in sizes]
    summed = sum(
        share * message_ref[slot(i, j), 32:64, :].astype(F32) for i, share in enumerate(shares)
    )
    return (summed / sum(shares)).astype(BF16)


def unpack_kernel(slot, gated, *refs):
    message_ref, out_ref = refs[0], refs[-1]
    for j in range(GROUPS):
        for i in range(SPLIT + 1):
            columns = head_columns(5 * j + i)
            rows = message_ref[slot(i, j), 0:32, :] if i < SPLIT else merged(message_ref, slot, j)
            if gated:
                rows = (refs[1][0:1, columns] * rows.astype(F32)).astype(BF16)
            out_ref[:, columns] = rows


def unpack(slot, message, gate=None):
    operands = [message] if gate is None else [message, gate]
    out_shape = jax.ShapeDtypeStruct((ROWS, 40 * HD), BF16)
    return call(functools.partial(unpack_kernel, slot, gate is not None), out_shape, operands)


def exchange(messages, group):
    return lax.all_to_all(messages, group, split_axis=0, concat_axis=0, tiled=True)


def shift(block, by):
    pairs = [(RING_ORDER[x], RING_ORDER[(x + by) % 4]) for x in range(4)]
    return lax.ppermute(block, RING, pairs)


def swap(block, axis, distance=1):
    size = dict(zip(AXES, SIZES))[axis]
    return lax.ppermute(block, axis, [(at, at ^ distance) for at in range(size)])


def pick(block, index):
    return lax.dynamic_index_in_dim(block, index, 0, keepdims=False)


def text_of_plane(text_context, chosen):
    xl, core = lax.axis_index("xl"), lax.axis_index("core")
    part = jax.ShapeDtypeStruct((2, 1280, HD), BF16)
    keep, send = call(pack_text_kernel, [part, part], (core.reshape(1), text_context), scalars=1)
    held = jnp.where(chosen % 2 == core, keep, swap(send, "core"))
    return jnp.where(chosen // 2 % 2 == xl, pick(held, xl), swap(pick(held, 1 - xl), "xl"))


def text_along_z(held, distance, chosen):
    agrees = (lax.axis_index("z") ^ (chosen // 4)) & distance == 0
    return jnp.where(agrees, held, swap(held, "z", distance))


def on_device(
    self_queries,
    self_keys,
    self_values,
    text_queries,
    text_context,
    sample,
    text_lengths,
    timestep,
    time_gates,
):
    chosen = sample[0]
    barrier = lax.optimization_barrier
    def message(rows):
        return jax.ShapeDtypeStruct((PEERS, rows, HD), BF16)

    blocks = call(pack_kernel, message(144), (self_keys, self_values, self_queries))
    text_blocks = call(pack_queries_kernel, message(64), (text_queries,))
    text = text_of_plane(text_context, chosen)
    queries = exchange(blocks, COLUMN)
    queries, text_blocks, text = barrier((queries, text_blocks, text))
    own = queries[:, 64:144]
    half = PEERS // 2

    up, down, other = shift(own, 1), shift(own, -1), swap(own, "core")
    text = text_along_z(text, 4, chosen)
    state = self_step(queries, [own], None)
    cross_queries = exchange(text_blocks, PLANE)
    up, down, other, text, state = barrier((up, down, other, text, state))

    far = [shift(up[:half], 1), shift(down[half:], -1)]
    other_up, other_down = swap(up, "core"), swap(down, "core")
    text = text_along_z(text, 2, chosen)
    state = self_step(queries, [other, up, down], state)
    far, other_up, other_down, text, state, cross_queries = barrier(
        (far, other_up, other_down, text, state, cross_queries)
    )

    other_far = [swap(x, "core") for x in far]
    text = text_along_z(text, 1, chosen)
    state = self_step(queries, [other_up, other_down, *far], state)
    other_far, text, state = barrier((other_far, text, state))

    place = lax.axis_index("xl") * 2 + lax.axis_index("core")
    cross = cross_step(jnp.stack([pick(text_lengths, chosen), place]), cross_queries, text)
    cross = exchange(cross, PLANE)
    result = exchange(self_step(queries, other_far, state, last=True), COLUMN)
    gate = lax.dynamic_slice_in_dim(time_gates, pick(timestep, chosen), 1, 0)
    return (unpack(self_slot, result, gate), unpack(cross_slot, cross))


def solution(mesh):
    fine = Mesh(mesh.devices.reshape(SIZES), AXES)
    rows = P(AXES, None)
    in_specs = (rows, rows, rows, rows, P(AXES[:3], None, None, AXES[3:]), P(), P(), P(), P())
    return jax.shard_map(on_device, mesh=fine, in_specs=in_specs, out_specs=(rows, rows), check_vma=False)
```

time: 187 us -> 156 us (0.83)
  blocking collectives: 29.1 us -> 0 us
  starting transfers between devices: 60 us -> 46.3 us
  waiting for transfers between devices: 41.7 us -> 52 us
  Pallas kernels: 44.7 us -> 40.8 us
  other arithmetic: 1.46 us -> 3.89 us
  local copies, waits for them, and re-layouts: 5.69 us -> 8.05 us
    all_gather x1 -> x0, blocking collectives: 29.1 us -> none  [text_of_sample(): return lax.all_gather(piece, 'z', axis=0, tiled=True)]
    ppermute x16 -> x14, starting transfers between devices: 24.6 us -> 13.9 us  [the longest x10 6.98 us: swap(): lax.ppermute(block, axis, [(at, at ^ distance) for at in range(size)])]
    all_to_all x5 -> x4, waiting for transfers between devices: 28.8 us -> 36 us  [exchange(): lax.all_to_all(messages, group, split_axis=0, concat_axis=0, tiled=True)]
    slice x1 -> x3, local copies, waits for them, and re-layouts: 0.04 us -> 5.4 us  [the longest x2 3.44 us: on_device(): far = [shift(up[:half], 1), shift(down[half:], -1)]]
    pallas_call x11 -> x10, Pallas kernels: 44.7 us -> 40.8 us  [call(): pl.pallas_call(kernel, out_shape=out_shape, grid=(1,), in_specs=in_specs,...]
    ppermute x16 -> x14, waiting for transfers between devices: 13 us -> 15.9 us  [the longest x10 13.1 us: swap(): lax.ppermute(block, axis, [(at, at ^ distance) for at in range(size)])]
    all_to_all x5 -> x4, starting transfers between devices: 35.4 us -> 32.5 us  [exchange(): lax.all_to_all(messages, group, split_axis=0, concat_axis=0, tiled=True)]
    unnamed x28 -> x10, local copies, waits for them, and re-layouts: 2.92 us -> 0.03 us
  transfers between devices with their start and end apart: 21 -> 18, of which waited for: 8 -> 9; matrix products, arithmetic and copies ran while one was open for 2% -> 8% of each run, Pallas kernels for 23% -> 21%
where the time goes in v2:
time: 156 us; the launch traced here: 154 us
  waiting for transfers between devices  52 us (33%)
  starting transfers between devices  46.3 us (30%)
  Pallas kernels  40.8 us (26%)
  local copies, waits for them, and re-layouts  8.05 us (5%)
  other arithmetic  3.89 us (2%)
  between operations  3.04 us (2%)
    pallas_call x10, Pallas kernels, call(): pl.pallas_call(kernel, out_shape=out_shape, grid=(1,), in_specs=in_specs,...  40.8 us
    all_to_all x4, waiting for transfers between devices, exchange(): lax.all_to_all(messages, group, split_axis=0, concat_axis=0, tiled=True)  36 us
    all_to_all x4, starting transfers between devices, exchange(): lax.all_to_all(messages, group, split_axis=0, concat_axis=0, tiled=True)  32.5 us
    ppermute x10, waiting for transfers between devices, swap(): lax.ppermute(block, axis, [(at, at ^ distance) for at in range(size)])  13.1 us
    ppermute x10, starting transfers between devices, swap(): lax.ppermute(block, axis, [(at, at ^ distance) for at in range(size)])  6.98 us
    ppermute x4, starting transfers between devices, shift(): return lax.ppermute(block, RING, pairs)  6.9 us
    slice x2, local copies, waits for them, and re-layouts, on_device(): far = [shift(up[:half], 1), shift(down[half:], -1)]  3.44 us
  transfers between devices with their start and end apart: 18, of which 9 were waited for; matrix products, arithmetic and copies ran while one was open for 8% of the time, Pallas kernels for 21%

profile of v2, /device:TPU:8, one launch (start us, length us, event | category | flops | bytes accessed | tf_op | source)
XLA Modules:
  0.0 154.0 jit_solution(14136328057664008194)
XLA Ops:
  0.6 2.5 %shard_map.104 = bf16[32,144,128]{2,1,0:T(8,128)(2,1)} custom-call(bf16[32,5120]{1,0:T(8,128)(2,1)} %keys_ref.1, bf16[32,5120]{1,0:T(8,128)(2,1)} %values_ref.1, bf16[32,5120]{1,0:T(8,128)(2,1)} %queries_ref.2), custom_call_target="tpu_custom_call" | custom-call | tf_op jit(solution)/shard_map/pallas_call | solution.py:39
  3.1 11.7 %all-to-all-start = ((bf16[32,144,128]{2,1,0:T(8,128)(2,1)}), bf16[32,144,128]{2,1,0:T(8,128)(2,1)}, u32[]{:S(2)}, u32[]{:S(2)}) async-start(bf16[32,144,128]{2,1,0:T(8,128)(2,1)} %shard_map.104), calls=%async_computation | async-start | bytes 2359296 | tf_op jit(solution)/shard_map/all_to_all | solution.py:339
  14.9 2.6 %shard_map.106 = (bf16[2,1280,128]{2,1,0:T(8,128)(2,1)}, bf16[2,1280,128]{2,1,0:T(8,128)(2,1)}) custom-call(s32[1]{0:T(128)} %bitcast.1.core_ref, bf16[1,2,512,640]{3,2,1,0:T(8,128)(2,1)} %text_ref.1), custom_call_target="tpu_custom_call" | custom-call | tf_op jit(solution)/shard_map/pallas_call | solution.py:39
  17.6 2.2 %collective-permute-done = bf16[2,1280,128]{2,1,0:T(8,128)(2,1)S(1)} collective-permute-done((bf16[2,1280,128]{2,1,0:T(8,128)(2,1)}, bf16[2,1280,128]{2,1,0:T(8,128)(2,1)S(1)}, u32[]{:S(2)}, u32[]{:S(2)}) %collective-permute-start) | collective-permute-done | bytes 655392 | tf_op jit(solution)/shard_map/ppermute | solution.py:349
  22.2 1.9 %shard_map.105 = bf16[32,64,128]{2,1,0:T(8,128)(2,1)} custom-call(bf16[32,5120]{1,0:T(8,128)(2,1)} %queries_ref.3), custom_call_target="tpu_custom_call" | custom-call | tf_op jit(solution)/shard_map/pallas_call | solution.py:39
  24.1 7.2 %collective-permute-done.1 = bf16[1280,128]{1,0:T(8,128)(2,1)} collective-permute-done((bf16[1280,128]{1,0:T(8,128)(2,1)}, bf16[1280,128]{1,0:T(8,128)(2,1)}, u32[]{:S(2)}, u32[]{:S(2)}) %collective-permute-start.1) | collective-permute-done | bytes 327712 | tf_op jit(solution)/shard_map/ppermute | solution.py:349
  32.1 13.7 %all-to-all-done.refs_0_ = bf16[32,144,128]{2,1,0:T(8,128)(2,1)} async-done(((bf16[32,144,128]{2,1,0:T(8,128)(2,1)}), bf16[32,144,128]{2,1,0:T(8,128)(2,1)}, u32[]{:S(2)}, u32[]{:S(2)}) %all-to-all-start) | async-done | bytes 1179680 | tf_op jit(solution)/shard_map/all_to_all | solution.py:339
  48.0 2.0 %slice.13.refs_1_ = bf16[32,80,128]{2,1,0:T(8,128)(2,1)} slice(bf16[32,144,128]{2,1,0:T(8,128)(2,1)} %all-to-all-done.refs_0_), slice={[0:32], [64:144], [0:128]} | slice | bytes 1310720 | tf_op jit(solution)/shard_map/slice | solution.py:390
  54.5 6.1 %all-to-all-start.1 = ((bf16[32,64,128]{2,1,0:T(8,128)(2,1)}), bf16[32,64,128]{2,1,0:T(8,128)(2,1)}, u32[]{:S(2)}, u32[]{:S(2)}) async-start(bf16[32,64,128]{2,1,0:T(8,128)(2,1)} %shard_map.105), calls=%async_computation.1 | async-start | bytes 1048576 | tf_op jit(solution)/shard_map/all_to_all | solution.py:339
  60.5 4.8 %shard_map.107 = (f32[1024,128]{1,0:T(8,128)}, f32[1024,128]{1,0:T(8,128)}, f32[1024,128]{1,0:T(8,128)}) custom-call(bf16[32,144,128]{2,1,0:T(8,128)(2,1)} %all-to-all-done.refs_0_, bf16[32,80,128]{2,1,0:T(8,128)(2,1)} %slice.13.refs_1_), custom_call_target="tpu_custom_call" | custom-call | flops 1342177280 | bytes 2752512 | tf_op jit(solution)/shard_map/pallas_call | solution.py:39
  66.4 2.6 %collective-permute-done.2.refs_2_ = bf16[32,80,128]{2,1,0:T(8,128)(2,1)} collective-permute-done((bf16[32,80,128]{2,1,0:T(8,128)(2,1)}, bf16[32,80,128]{2,1,0:T(8,128)(2,1)}, u32[]{:S(2)}, u32[]{:S(2)}) %collective-permute-start.2) | collective-permute-done | bytes 655392 | tf_op jit(solution)/shard_map/ppermute | solution.py:344
  73.1 2.8 %collective-permute-start.10 = (bf16[1280,128]{1,0:T(8,128)(2,1)S(1)}, bf16[1280,128]{1,0:T(8,128)(2,1)}, u32[]{:S(2)}, u32[]{:S(2)}) collective-permute-start(bf16[1280,128]{1,0:T(8,128)(2,1)S(1)} %broadcast_select_fusion.3), channel_id=1, source_target_pairs={{0,64},{32,96},{64,0},{96,32},{128,192},{160,224},{192,128},{224,1... | collective-permute-start | bytes 983048 | tf_op jit(solution)/shard_map/ppermute | solution.py:349
  77.1 2.5 %collective-permute-start.7 = (bf16[16,80,128]{2,1,0:T(8,128)(2,1)}, bf16[16,80,128]{2,1,0:T(8,128)(2,1)}, u32[]{:S(2)}, u32[]{:S(2)}) collective-permute-start(bf16[16,80,128]{2,1,0:T(8,128)(2,1)} %slice.15), channel_id=1, source_target_pairs={{0,20},{16,0},{4,16},{20,4},{1,21},{17,1},{5,17},{21,5},{2,22},{18... | collective-permute-start | bytes 983048 | tf_op jit(solution)/shard_map/ppermute | solution.py:344
  79.6 8.1 %shard_map.108 = (f32[1024,128]{1,0:T(8,128)}, f32[1024,128]{1,0:T(8,128)}, f32[1024,128]{1,0:T(8,128)}) custom-call(bf16[32,144,128]{2,1,0:T(8,128)(2,1)} %all-to-all-done.refs_0_, bf16[32,80,128]{2,1,0:T(8,128)(2,1)} %collective-permute-done.4.refs_1_, bf16[32,80,128]{2,1,0:T(8,128)(2,1)} %collective-permute-done.2.refs_2_, ...), custom_call_target="tpu_custom_call" | custom-call | flops 4026531840 | bytes 4063232 | tf_op jit(solution)/shard_map/pallas_call | solution.py:39
  87.7 2.7 %collective-permute-done.10 = bf16[1280,128]{1,0:T(8,128)(2,1)} collective-permute-done((bf16[1280,128]{1,0:T(8,128)(2,1)S(1)}, bf16[1280,128]{1,0:T(8,128)(2,1)}, u32[]{:S(2)}, u32[]{:S(2)}) %collective-permute-start.10) | collective-permute-done | bytes 327712 | tf_op jit(solution)/shard_map/ppermute | solution.py:349
  91.2 8.0 %shard_map.109 = (f32[1024,128]{1,0:T(8,128)}, f32[1024,128]{1,0:T(8,128)}, f32[1024,128]{1,0:T(8,128)}) custom-call(bf16[32,144,128]{2,1,0:T(8,128)(2,1)} %all-to-all-done.refs_0_, bf16[32,80,128]{2,1,0:T(8,128)(2,1)} %collective-permute-done.8.refs_1_, bf16[32,80,128]{2,1,0:T(8,128)(2,1)} %collective-permute-done.9.refs_2_, ...), custom_call_target="tpu_custom_call" | custom-call | flops 4026531840 | bytes 4063232 | tf_op jit(solution)/shard_map/pallas_call | solution.py:39
  101.0 3.8 %shard_map.112 = bf16[32,80,128]{2,1,0:T(8,128)(2,1)} custom-call(s32[2]{0:T(128)} %pad_add_fusion.scalars_ref, bf16[32,64,128]{2,1,0:T(8,128)(2,1)} %all-to-all-done.1.queries_ref, bf16[1280,128]{1,0:T(8,128)(2,1)} %broadcast_select_fusion.1.text_ref), custom_call_target="tpu_custom_call" | custom-call | flops 671088640 | bytes 2097152 | tf_op jit(solution)/shard_map/pallas_call | solution.py:39
  104.7 7.5 %all-to-all-start.3 = ((bf16[32,80,128]{2,1,0:T(8,128)(2,1)}), bf16[32,80,128]{2,1,0:T(8,128)(2,1)S(1)}, u32[]{:S(2)}, u32[]{:S(2)}) async-start(bf16[32,80,128]{2,1,0:T(8,128)(2,1)} %shard_map.112), calls=%async_computation.3 | async-start | bytes 1310720 | tf_op jit(solution)/shard_map/all_to_all | solution.py:339
  112.2 5.0 %shard_map.110 = bf16[32,80,128]{2,1,0:T(8,128)(2,1)} custom-call(bf16[32,144,128]{2,1,0:T(8,128)(2,1)} %all-to-all-done.refs_0_, bf16[16,80,128]{2,1,0:T(8,128)(2,1)} %collective-permute-done.11.refs_1_, bf16[16,80,128]{2,1,0:T(8,128)(2,1)} %collective-permute-done.12.refs_2_, f32[1024,128]{1,0:T(8,128)} %get-tuple-element.69.refs_3_, ...), custom_call_target="tpu_custom_call" | custom-call | flops 1342177280 | bytes 2752512 | tf_op jit(solution)/shard_map/pallas_call | solution.py:39
  117.2 7.1 %all-to-all-done.3.refs_0_ = bf16[32,80,128]{2,1,0:T(8,128)(2,1)S(1)} async-done(((bf16[32,80,128]{2,1,0:T(8,128)(2,1)}), bf16[32,80,128]{2,1,0:T(8,128)(2,1)S(1)}, u32[]{:S(2)}, u32[]{:S(2)}) %all-to-all-start.3) | async-done | bytes 655392 | tf_op jit(solution)/shard_map/all_to_all | solution.py:339
  124.3 7.2 %all-to-all-start.2 = ((bf16[32,80,128]{2,1,0:T(8,128)(2,1)}), bf16[32,80,128]{2,1,0:T(8,128)(2,1)}, u32[]{:S(2)}, u32[]{:S(2)}) async-start(bf16[32,80,128]{2,1,0:T(8,128)(2,1)} %shard_map.110), calls=%async_computation.2 | async-start | bytes 1310720 | tf_op jit(solution)/shard_map/all_to_all | solution.py:339
  134.7 2.1 %shard_map.113 = bf16[32,5120]{1,0:T(8,128)(2,1)} custom-call(bf16[32,80,128]{2,1,0:T(8,128)(2,1)} %copy-done.1), custom_call_target="tpu_custom_call" | custom-call | tf_op jit(solution)/shard_map/pallas_call | solution.py:39
  136.8 15.2 %all-to-all-done.2.refs_0_ = bf16[32,80,128]{2,1,0:T(8,128)(2,1)} async-done(((bf16[32,80,128]{2,1,0:T(8,128)(2,1)}), bf16[32,80,128]{2,1,0:T(8,128)(2,1)}, u32[]{:S(2)}, u32[]{:S(2)}) %all-to-all-start.2) | async-done | bytes 655392 | tf_op jit(solution)/shard_map/all_to_all | solution.py:339
  151.9 2.1 %shard_map.111 = bf16[32,5120]{1,0:T(8,128)(2,1)} custom-call(bf16[32,80,128]{2,1,0:T(8,128)(2,1)} %all-to-all-done.2.refs_0_, f32[1,5120]{1,0:T(1,128)} %constant_dynamic-slice_fusion.refs_1_), custom_call_target="tpu_custom_call" | custom-call | tf_op jit(solution)/shard_map/pallas_call | solution.py:39
  (45 shorter events, 19.8 us)
Async XLA Ops:
  0.6 133.4 %copy-start = (f32[50,5120]{1,0:T(8,128)S(1)}, f32[50,5120]{1,0:T(8,128)}, u32[]{:S(2)}) copy-start(f32[50,5120]{1,0:T(8,128)} %param.17) | copy-start | bytes 3072004
  3.1 42.7 %all-to-all-start = ((bf16[32,144,128]{2,1,0:T(8,128)(2,1)}), bf16[32,144,128]{2,1,0:T(8,128)(2,1)}, u32[]{:S(2)}, u32[]{:S(2)}) async-start(bf16[32,144,128]{2,1,0:T(8,128)(2,1)} %shard_map.104), calls=%async_computation | async-start | bytes 2359296 | tf_op jit(solution)/shard_map/all_to_all | solution.py:339
  14.9 2.6 %copy-start.2 = (s32[32]{0:T(128)S(1)}, s32[32]{0:T(128)}, u32[]{:S(2)}) copy-start(s32[32]{0:T(128)} %param.14) | copy-start | bytes 388
  17.5 2.3 %collective-permute-start = (bf16[2,1280,128]{2,1,0:T(8,128)(2,1)}, bf16[2,1280,128]{2,1,0:T(8,128)(2,1)S(1)}, u32[]{:S(2)}, u32[]{:S(2)}) collective-permute-start(bf16[2,1280,128]{2,1,0:T(8,128)(2,1)} %get-tuple-element.39), channel_id=1, source_target_pairs={{0,8},{8,0},{1,9},{9,1},{2,10},{10,2},{3,11},{11,3},{4,12},{12,4},... | collective-permute-start | bytes 1966088 | tf_op jit(solution)/shard_map/ppermute | solution.py:349
  19.9 27.5 %copy-start.3 = (s32[32]{0:T(128)S(1)}, s32[32]{0:T(128)}, u32[]{:S(2)}) copy-start(s32[32]{0:T(128)} %param.15) | copy-start | bytes 388
  20.6 10.6 %collective-permute-start.1 = (bf16[1280,128]{1,0:T(8,128)(2,1)}, bf16[1280,128]{1,0:T(8,128)(2,1)}, u32[]{:S(2)}, u32[]{:S(2)}) collective-permute-start(bf16[1280,128]{1,0:T(8,128)(2,1)} %dynamic-slice_bitcast_fusion), channel_id=1, source_target_pairs={{0,16},{16,0},{1,17},{17,1},{2,18},{18,2},{3,19},{19,3},{4,20},{20... | collective-permute-start | bytes 983048 | tf_op jit(solution)/shard_map/ppermute | solution.py:349
  45.8 19.6 %collective-permute-start.5 = (bf16[1280,128]{1,0:T(8,128)(2,1)}, bf16[1280,128]{1,0:T(8,128)(2,1)S(1)}, u32[]{:S(2)}, u32[]{:S(2)}) collective-permute-start(bf16[1280,128]{1,0:T(8,128)(2,1)} %bitcast_select_fusion), channel_id=1, source_target_pairs={{0,128},{32,160},{64,192},{96,224},{128,0},{160,32},{192,64},{224,... | collective-permute-start | bytes 983048 | tf_op jit(solution)/shard_map/ppermute | solution.py:349
  50.0 19.0 %collective-permute-start.2 = (bf16[32,80,128]{2,1,0:T(8,128)(2,1)}, bf16[32,80,128]{2,1,0:T(8,128)(2,1)}, u32[]{:S(2)}, u32[]{:S(2)}) collective-permute-start(bf16[32,80,128]{2,1,0:T(8,128)(2,1)} %slice.13.refs_1_), channel_id=1, source_target_pairs={{0,16},{16,4},{4,20},{20,0},{1,17},{17,5},{5,21},{21,1},{2,18},{18... | collective-permute-start | bytes 1966088 | tf_op jit(solution)/shard_map/ppermute | solution.py:344
  51.5 17.7 %collective-permute-start.3 = (bf16[32,80,128]{2,1,0:T(8,128)(2,1)}, bf16[32,80,128]{2,1,0:T(8,128)(2,1)}, u32[]{:S(2)}, u32[]{:S(2)}) collective-permute-start(bf16[32,80,128]{2,1,0:T(8,128)(2,1)} %slice.13.refs_1_), channel_id=1, source_target_pairs={{0,20},{16,0},{4,16},{20,4},{1,21},{17,1},{5,17},{21,5},{2,22},{18... | collective-permute-start | bytes 1966088 | tf_op jit(solution)/shard_map/ppermute | solution.py:344
  53.2 16.0 %collective-permute-start.4 = (bf16[32,80,128]{2,1,0:T(8,128)(2,1)}, bf16[32,80,128]{2,1,0:T(8,128)(2,1)}, u32[]{:S(2)}, u32[]{:S(2)}) collective-permute-start(bf16[32,80,128]{2,1,0:T(8,128)(2,1)} %slice.13.refs_1_), channel_id=1, source_target_pairs={{0,8},{8,0},{1,9},{9,1},{2,10},{10,2},{3,11},{11,3},{4,12},{12,4},... | collective-permute-start | bytes 1966088 | tf_op jit(solution)/shard_map/ppermute | solution.py:349
  54.5 36.0 %all-to-all-start.1 = ((bf16[32,64,128]{2,1,0:T(8,128)(2,1)}), bf16[32,64,128]{2,1,0:T(8,128)(2,1)}, u32[]{:S(2)}, u32[]{:S(2)}) async-start(bf16[32,64,128]{2,1,0:T(8,128)(2,1)} %shard_map.105), calls=%async_computation.1 | async-start | bytes 1048576 | tf_op jit(solution)/shard_map/all_to_all | solution.py:339
  70.9 19.6 %collective-permute-start.8 = (bf16[32,80,128]{2,1,0:T(8,128)(2,1)}, bf16[32,80,128]{2,1,0:T(8,128)(2,1)}, u32[]{:S(2)}, u32[]{:S(2)}) collective-permute-start(bf16[32,80,128]{2,1,0:T(8,128)(2,1)} %collective-permute-done.2.refs_2_), channel_id=1, source_target_pairs={{0,8},{8,0},{1,9},{9,1},{2,10},{10,2},{3,11},{11,3},{4,12},{12,4},... | collective-permute-start | bytes 1966088 | tf_op jit(solution)/shard_map/ppermute | solution.py:349
  72.6 17.9 %collective-permute-start.9 = (bf16[32,80,128]{2,1,0:T(8,128)(2,1)}, bf16[32,80,128]{2,1,0:T(8,128)(2,1)}, u32[]{:S(2)}, u32[]{:S(2)}) collective-permute-start(bf16[32,80,128]{2,1,0:T(8,128)(2,1)} %collective-permute-done.3.refs_3_), channel_id=1, source_target_pairs={{0,8},{8,0},{1,9},{9,1},{2,10},{10,2},{3,11},{11,3},{4,12},{12,4},... | collective-permute-start | bytes 1966088 | tf_op jit(solution)/shard_map/ppermute | solution.py:349
  73.1 17.3 %collective-permute-start.10 = (bf16[1280,128]{1,0:T(8,128)(2,1)S(1)}, bf16[1280,128]{1,0:T(8,128)(2,1)}, u32[]{:S(2)}, u32[]{:S(2)}) collective-permute-start(bf16[1280,128]{1,0:T(8,128)(2,1)S(1)} %broadcast_select_fusion.3), channel_id=1, source_target_pairs={{0,64},{32,96},{64,0},{96,32},{128,192},{160,224},{192,128},{224,1... | collective-permute-start | bytes 983048 | tf_op jit(solution)/shard_map/ppermute | solution.py:349
  76.0 14.5 %collective-permute-start.6 = (bf16[16,80,128]{2,1,0:T(8,128)(2,1)}, bf16[16,80,128]{2,1,0:T(8,128)(2,1)}, u32[]{:S(2)}, u32[]{:S(2)}) collective-permute-start(bf16[16,80,128]{2,1,0:T(8,128)(2,1)} %slice.14), channel_id=1, source_target_pairs={{0,16},{16,4},{4,20},{20,0},{1,17},{17,5},{5,21},{21,1},{2,18},{18... | collective-permute-start | bytes 983048 | tf_op jit(solution)/shard_map/ppermute | solution.py:344
  77.1 13.3 %collective-permute-start.7 = (bf16[16,80,128]{2,1,0:T(8,128)(2,1)}, bf16[16,80,128]{2,1,0:T(8,128)(2,1)}, u32[]{:S(2)}, u32[]{:S(2)}) collective-permute-start(bf16[16,80,128]{2,1,0:T(8,128)(2,1)} %slice.15), channel_id=1, source_target_pairs={{0,20},{16,0},{4,16},{20,4},{1,21},{17,1},{5,17},{21,5},{2,22},{18... | collective-permute-start | bytes 983048 | tf_op jit(solution)/shard_map/ppermute | solution.py:344
  90.5 9.7 %collective-permute-start.13 = (bf16[1280,128]{1,0:T(8,128)(2,1)S(1)}, bf16[1280,128]{1,0:T(8,128)(2,1)S(1)}, u32[]{:S(2)}, u32[]{:S(2)}) collective-permute-start(bf16[1280,128]{1,0:T(8,128)(2,1)S(1)} %broadcast_select_fusion.2), channel_id=1, source_target_pairs={{0,32},{32,0},{64,96},{96,64},{128,160},{160,128},{192,224},{224,1... | collective-permute-start | bytes 983048 | tf_op jit(solution)/shard_map/ppermute | solution.py:349
  90.6 10.4 %collective-permute-start.11 = (bf16[16,80,128]{2,1,0:T(8,128)(2,1)}, bf16[16,80,128]{2,1,0:T(8,128)(2,1)}, u32[]{:S(2)}, u32[]{:S(2)}) collective-permute-start(bf16[16,80,128]{2,1,0:T(8,128)(2,1)} %collective-permute-done.6.refs_3_), channel_id=1, source_target_pairs={{0,8},{8,0},{1,9},{9,1},{2,10},{10,2},{3,11},{11,3},{4,12},{12,4},... | collective-permute-start | bytes 983048 | tf_op jit(solution)/shard_map/ppermute | solution.py:349
  90.7 10.3 %collective-permute-start.12 = (bf16[16,80,128]{2,1,0:T(8,128)(2,1)}, bf16[16,80,128]{2,1,0:T(8,128)(2,1)}, u32[]{:S(2)}, u32[]{:S(2)}) collective-permute-start(bf16[16,80,128]{2,1,0:T(8,128)(2,1)} %collective-permute-done.7.refs_4_), channel_id=1, source_target_pairs={{0,8},{8,0},{1,9},{9,1},{2,10},{10,2},{3,11},{11,3},{4,12},{12,4},... | collective-permute-start | bytes 983048 | tf_op jit(solution)/shard_map/ppermute | solution.py:349
  104.7 19.6 %all-to-all-start.3 = ((bf16[32,80,128]{2,1,0:T(8,128)(2,1)}), bf16[32,80,128]{2,1,0:T(8,128)(2,1)S(1)}, u32[]{:S(2)}, u32[]{:S(2)}) async-start(bf16[32,80,128]{2,1,0:T(8,128)(2,1)} %shard_map.112), calls=%async_computation.3 | async-start | bytes 1310720 | tf_op jit(solution)/shard_map/all_to_all | solution.py:339
  117.2 14.3 %copy-start.4 = (s32[32]{0:T(128)S(1)}, s32[32]{0:T(128)}, u32[]{:S(2)}) copy-start(s32[32]{0:T(128)} %param.16) | copy-start | bytes 388
  124.3 10.3 %copy-start.1 = (bf16[32,80,128]{2,1,0:T(8,128)(2,1)}, bf16[32,80,128]{2,1,0:T(8,128)(2,1)S(1)}, u32[]{:S(2)}) copy-start(bf16[32,80,128]{2,1,0:T(8,128)(2,1)S(1)} %all-to-all-done.3.refs_0_) | copy-start | bytes 1966084
  124.3 27.6 %all-to-all-start.2 = ((bf16[32,80,128]{2,1,0:T(8,128)(2,1)}), bf16[32,80,128]{2,1,0:T(8,128)(2,1)}, u32[]{:S(2)}, u32[]{:S(2)}) async-start(bf16[32,80,128]{2,1,0:T(8,128)(2,1)} %shard_map.110), calls=%async_computation.2 | async-start | bytes 1310720 | tf_op jit(solution)/shard_map/all_to_all | solution.py:339

commit v3 on v2

--- a/solution.py
+++ b/solution.py
@@ -26,7 +26,7 @@
 SCALE = math.log2(math.e) / math.sqrt(HD)
 F32 = jnp.float32
 BF16 = jnp.bfloat16
-VMEM_LIMIT = 62 * 1024 * 1024
+VMEM_LIMIT = 63 * 1024 * 1024
 
 
 def whole_block(shape):
@@ -164,22 +164,18 @@
 
 def fold_lazily(scaled, keys, values, state):
     top, total, summed = state
-    excess = None
     for at in range(0, keys.shape[0], CHUNK):
         part = slice(at, min(at + CHUNK, keys.shape[0]))
-        scores = products(scaled, keys[part]) - top
-        most = jnp.max(scores.reshape(-1, 8, scores.shape[1]), axis=0)
-        most = functools.reduce(jnp.maximum, [most[:, t : t + HD] for t in range(0, most.shape[1], HD)])
-        excess = most if excess is None else jnp.maximum(excess, most)
-        term = jnp.dot(jnp.exp2(scores).astype(BF16), values[part], preferred_element_type=F32)
+        weights = jnp.exp2(products(scaled, keys[part]) - top).astype(BF16)
+        term = jnp.dot(weights, values[part], preferred_element_type=F32)
         total = total + term[:, HD : HD + 1]
         summed = summed + term[:, :HD]
-    return (top, total, summed), excess
+    return top, total, summed
 
 
 SENDERS = 8
 CHUNK = 512
-MOST = 64.0
+MOST = 2.0**64
 
 
 def keys_and_values(shard_refs):
@@ -228,21 +224,21 @@
         return pl.ds(index * SENDERS, SENDERS), pl.ds(start, block)
 
     pairs = keys_and_values(shard_refs)
-    excess = None
+    most = None
     for index in range(PEERS // SENDERS):
         senders, rows = places(index)
         scaled = queries_of(senders)
         if first:
             write(senders, rows, *(fold(products(q, k), v, None) for q, (k, v) in zip(scaled, pairs)))
             continue
-        done = [fold_lazily(q, k, v, state) for q, (k, v), state in zip(scaled, pairs, states_of(rows))]
-        write(senders, rows, done[0][0], done[1][0])
-        for _, most in done:
-            excess = most if excess is None else jnp.maximum(excess, most)
+        found = [fold_lazily(q, k, v, state) for q, (k, v), state in zip(scaled, pairs, states_of(rows))]
+        write(senders, rows, *found)
+        totals = jnp.maximum(found[0][1], found[1][1])
+        most = totals if most is None else jnp.maximum(most, totals)
     if first:
         return
 
-    @pl.when(jnp.max(excess) > MOST)
+    @pl.when(jnp.max(most) > MOST)
     def _():
         again = keys_and_values(shard_refs)
 
@@ -387,7 +383,7 @@
     text = text_of_plane(text_context, chosen)
     queries = exchange(blocks, COLUMN)
     queries, text_blocks, text = barrier((queries, text_blocks, text))
-    own = queries[:, 64:144]
+    own, text = barrier((queries[:, 64:144], text))
     half = PEERS // 2
 
     up, down, other = shift(own, 1), shift(own, -1), swap(own, "core")

time: 156 us -> 155 us (level)
  other arithmetic: 3.89 us -> 2.2 us
  transfers between devices with their start and end apart: 18 -> 18, of which waited for: 9 -> 9; matrix products, arithmetic and copies ran while one was open for 8% -> 5% of each run, Pallas kernels for 21% -> 21%
where the time goes in v3:
time: 155 us; the launch traced here: 154 us
  waiting for transfers between devices  52.7 us (34%)
  starting transfers between devices  46.5 us (30%)
  Pallas kernels  41.3 us (27%)
  local copies, waits for them, and re-layouts  8.18 us (5%)
  between operations  3.03 us (2%)
  other arithmetic  2.2 us (1%)
    pallas_call x10, Pallas kernels, call(): pl.pallas_call(kernel, out_shape=out_shape, grid=(1,), in_specs=in_specs,...  41.3 us
    all_to_all x4, waiting for transfers between devices, exchange(): lax.all_to_all(messages, group, split_axis=0, concat_axis=0, tiled=True)  36.6 us
    all_to_all x4, starting transfers between devices, exchange(): lax.all_to_all(messages, group, split_axis=0, concat_axis=0, tiled=True)  32.5 us
    ppermute x10, waiting for transfers between devices, swap(): lax.ppermute(block, axis, [(at, at ^ distance) for at in range(size)])  12.4 us
    ppermute x10, starting transfers between devices, swap(): lax.ppermute(block, axis, [(at, at ^ distance) for at in range(size)])  7.07 us
    ppermute x4, starting transfers between devices, shift(): return lax.ppermute(block, RING, pairs)  6.9 us
    ppermute x4, waiting for transfers between devices, shift(): return lax.ppermute(block, RING, pairs)  3.73 us
    slice x2, local copies, waits for them, and re-layouts, on_device(): far = [shift(up[:half], 1), shift(down[half:], -1)]  3.44 us
  transfers between devices with their start and end apart: 18, of which 9 were waited for; matrix products, arithmetic and copies ran while one was open for 5% of the time, Pallas kernels for 21%

profile of v3, /device:TPU:8, one launch (start us, length us, event | category | flops | bytes accessed | tf_op | source)
XLA Modules:
  0.0 154.0 jit_solution(6196827730638876032)
XLA Ops:
  0.6 2.4 %shard_map.104 = bf16[32,144,128]{2,1,0:T(8,128)(2,1)} custom-call(bf16[32,5120]{1,0:T(8,128)(2,1)} %keys_ref.1, bf16[32,5120]{1,0:T(8,128)(2,1)} %values_ref.1, bf16[32,5120]{1,0:T(8,128)(2,1)} %queries_ref.2), custom_call_target="tpu_custom_call" | custom-call | tf_op jit(solution)/shard_map/pallas_call | solution.py:39
  3.0 11.7 %all-to-all-start = ((bf16[32,144,128]{2,1,0:T(8,128)(2,1)}), bf16[32,144,128]{2,1,0:T(8,128)(2,1)}, u32[]{:S(2)}, u32[]{:S(2)}) async-start(bf16[32,144,128]{2,1,0:T(8,128)(2,1)} %shard_map.104), calls=%async_computation | async-start | bytes 2359296 | tf_op jit(solution)/shard_map/all_to_all | solution.py:335
  14.8 2.6 %shard_map.106 = (bf16[2,1280,128]{2,1,0:T(8,128)(2,1)}, bf16[2,1280,128]{2,1,0:T(8,128)(2,1)}) custom-call(s32[1]{0:T(128)} %bitcast.1.core_ref, bf16[1,2,512,640]{3,2,1,0:T(8,128)(2,1)} %text_ref.1), custom_call_target="tpu_custom_call" | custom-call | tf_op jit(solution)/shard_map/pallas_call | solution.py:39
  17.6 2.2 %collective-permute-done = bf16[2,1280,128]{2,1,0:T(8,128)(2,1)S(1)} collective-permute-done((bf16[2,1280,128]{2,1,0:T(8,128)(2,1)}, bf16[2,1280,128]{2,1,0:T(8,128)(2,1)S(1)}, u32[]{:S(2)}, u32[]{:S(2)}) %collective-permute-start) | collective-permute-done | bytes 655392 | tf_op jit(solution)/shard_map/ppermute | solution.py:345
  21.5 1.9 %shard_map.105 = bf16[32,64,128]{2,1,0:T(8,128)(2,1)} custom-call(bf16[32,5120]{1,0:T(8,128)(2,1)} %queries_ref.3), custom_call_target="tpu_custom_call" | custom-call | tf_op jit(solution)/shard_map/pallas_call | solution.py:39
  23.4 7.0 %collective-permute-done.1 = bf16[1280,128]{1,0:T(8,128)(2,1)} collective-permute-done((bf16[1280,128]{1,0:T(8,128)(2,1)S(1)}, bf16[1280,128]{1,0:T(8,128)(2,1)}, u32[]{:S(2)}, u32[]{:S(2)}) %collective-permute-start.1) | collective-permute-done | bytes 327712 | tf_op jit(solution)/shard_map/ppermute | solution.py:345
  30.4 15.3 %all-to-all-done.refs_0_ = bf16[32,144,128]{2,1,0:T(8,128)(2,1)} async-done(((bf16[32,144,128]{2,1,0:T(8,128)(2,1)}), bf16[32,144,128]{2,1,0:T(8,128)(2,1)}, u32[]{:S(2)}, u32[]{:S(2)}) %all-to-all-start) | async-done | bytes 1179680 | tf_op jit(solution)/shard_map/all_to_all | solution.py:335
  45.7 2.0 %slice.13.refs_1_ = bf16[32,80,128]{2,1,0:T(8,128)(2,1)} slice(bf16[32,144,128]{2,1,0:T(8,128)(2,1)} %all-to-all-done.refs_0_), slice={[0:32], [64:144], [0:128]} | slice | bytes 1310720 | tf_op jit(solution)/shard_map/slice | solution.py:386
  54.3 6.1 %all-to-all-start.1 = ((bf16[32,64,128]{2,1,0:T(8,128)(2,1)}), bf16[32,64,128]{2,1,0:T(8,128)(2,1)}, u32[]{:S(2)}, u32[]{:S(2)}) async-start(bf16[32,64,128]{2,1,0:T(8,128)(2,1)} %shard_map.105), calls=%async_computation.1 | async-start | bytes 1048576 | tf_op jit(solution)/shard_map/all_to_all | solution.py:335
  60.4 4.8 %shard_map.107 = (f32[1024,128]{1,0:T(8,128)}, f32[1024,128]{1,0:T(8,128)}, f32[1024,128]{1,0:T(8,128)}) custom-call(bf16[32,144,128]{2,1,0:T(8,128)(2,1)} %all-to-all-done.refs_0_, bf16[32,80,128]{2,1,0:T(8,128)(2,1)} %slice.13.refs_1_), custom_call_target="tpu_custom_call" | custom-call | flops 1342177280 | bytes 2752512 | tf_op jit(solution)/shard_map/pallas_call | solution.py:39
  65.3 3.6 %collective-permute-done.2.refs_2_ = bf16[32,80,128]{2,1,0:T(8,128)(2,1)} collective-permute-done((bf16[32,80,128]{2,1,0:T(8,128)(2,1)}, bf16[32,80,128]{2,1,0:T(8,128)(2,1)}, u32[]{:S(2)}, u32[]{:S(2)}) %collective-permute-start.2) | collective-permute-done | bytes 655392 | tf_op jit(solution)/shard_map/ppermute | solution.py:340
  73.0 2.8 %collective-permute-start.10 = (bf16[1280,128]{1,0:T(8,128)(2,1)S(1)}, bf16[1280,128]{1,0:T(8,128)(2,1)S(1)}, u32[]{:S(2)}, u32[]{:S(2)}) collective-permute-start(bf16[1280,128]{1,0:T(8,128)(2,1)S(1)} %broadcast_select_fusion.3), channel_id=1, source_target_pairs={{0,64},{32,96},{64,0},{96,32},{128,192},{160,224},{192,128},{224,1... | collective-permute-start | bytes 983048 | tf_op jit(solution)/shard_map/ppermute | solution.py:345
  77.0 2.5 %collective-permute-start.7 = (bf16[16,80,128]{2,1,0:T(8,128)(2,1)}, bf16[16,80,128]{2,1,0:T(8,128)(2,1)}, u32[]{:S(2)}, u32[]{:S(2)}) collective-permute-start(bf16[16,80,128]{2,1,0:T(8,128)(2,1)} %slice.15), channel_id=1, source_target_pairs={{0,20},{16,0},{4,16},{20,4},{1,21},{17,1},{5,17},{21,5},{2,22},{18... | collective-permute-start | bytes 983048 | tf_op jit(solution)/shard_map/ppermute | solution.py:340
  79.5 8.2 %shard_map.108 = (f32[1024,128]{1,0:T(8,128)}, f32[1024,128]{1,0:T(8,128)}, f32[1024,128]{1,0:T(8,128)}) custom-call(bf16[32,144,128]{2,1,0:T(8,128)(2,1)} %all-to-all-done.refs_0_, bf16[32,80,128]{2,1,0:T(8,128)(2,1)} %collective-permute-done.4.refs_1_, bf16[32,80,128]{2,1,0:T(8,128)(2,1)} %collective-permute-done.2.refs_2_, ...), custom_call_target="tpu_custom_call" | custom-call | flops 4026531840 | bytes 4063232 | tf_op jit(solution)/shard_map/pallas_call | solution.py:39
  87.7 2.4 %collective-permute-done.10 = bf16[1280,128]{1,0:T(8,128)(2,1)S(1)} collective-permute-done((bf16[1280,128]{1,0:T(8,128)(2,1)S(1)}, bf16[1280,128]{1,0:T(8,128)(2,1)S(1)}, u32[]{:S(2)}, u32[]{:S(2)}) %collective-permute-start.10) | collective-permute-done | bytes 327712 | tf_op jit(solution)/shard_map/ppermute | solution.py:345
  90.9 8.2 %shard_map.109 = (f32[1024,128]{1,0:T(8,128)}, f32[1024,128]{1,0:T(8,128)}, f32[1024,128]{1,0:T(8,128)}) custom-call(bf16[32,144,128]{2,1,0:T(8,128)(2,1)} %all-to-all-done.refs_0_, bf16[32,80,128]{2,1,0:T(8,128)(2,1)} %collective-permute-done.8.refs_1_, bf16[32,80,128]{2,1,0:T(8,128)(2,1)} %collective-permute-done.9.refs_2_, ...), custom_call_target="tpu_custom_call" | custom-call | flops 4026531840 | bytes 4063232 | tf_op jit(solution)/shard_map/pallas_call | solution.py:39
  100.7 3.9 %shard_map.112 = bf16[32,80,128]{2,1,0:T(8,128)(2,1)} custom-call(s32[2]{0:T(128)} %pad_add_fusion.scalars_ref, bf16[32,64,128]{2,1,0:T(8,128)(2,1)} %all-to-all-done.1.queries_ref, bf16[1280,128]{1,0:T(8,128)(2,1)} %broadcast_select_fusion.1.text_ref), custom_call_target="tpu_custom_call" | custom-call | flops 671088640 | bytes 2097152 | tf_op jit(solution)/shard_map/pallas_call | solution.py:39
  104.6 7.5 %all-to-all-start.3 = ((bf16[32,80,128]{2,1,0:T(8,128)(2,1)}), bf16[32,80,128]{2,1,0:T(8,128)(2,1)S(1)}, u32[]{:S(2)}, u32[]{:S(2)}) async-start(bf16[32,80,128]{2,1,0:T(8,128)(2,1)} %shard_map.112), calls=%async_computation.3 | async-start | bytes 1310720 | tf_op jit(solution)/shard_map/all_to_all | solution.py:335
  112.1 5.1 %shard_map.110 = bf16[32,80,128]{2,1,0:T(8,128)(2,1)} custom-call(bf16[32,144,128]{2,1,0:T(8,128)(2,1)} %all-to-all-done.refs_0_, bf16[16,80,128]{2,1,0:T(8,128)(2,1)} %copy-done.4, bf16[16,80,128]{2,1,0:T(8,128)(2,1)} %collective-permute-done.12.refs_2_, f32[1024,128]{1,0:T(8,128)} %get-tuple-element.73.refs_3_, f32[1024,128]{1,0:T(8,128)} %get-tuple-element.74.refs_4_, ...), custom_call_target="tpu_custom_call" | custom-call | flops 1342177280 | bytes 2752512 | tf_op jit(solution)/shard_map/pallas_call | solution.py:39
  117.2 7.0 %all-to-all-done.3.refs_0_ = bf16[32,80,128]{2,1,0:T(8,128)(2,1)S(1)} async-done(((bf16[32,80,128]{2,1,0:T(8,128)(2,1)}), bf16[32,80,128]{2,1,0:T(8,128)(2,1)S(1)}, u32[]{:S(2)}, u32[]{:S(2)}) %all-to-all-start.3) | async-done | bytes 655392 | tf_op jit(solution)/shard_map/all_to_all | solution.py:335
  124.2 7.2 %all-to-all-start.2 = ((bf16[32,80,128]{2,1,0:T(8,128)(2,1)}), bf16[32,80,128]{2,1,0:T(8,128)(2,1)}, u32[]{:S(2)}, u32[]{:S(2)}) async-start(bf16[32,80,128]{2,1,0:T(8,128)(2,1)} %shard_map.110), calls=%async_computation.2 | async-start | bytes 1310720 | tf_op jit(solution)/shard_map/all_to_all | solution.py:335
  135.5 2.1 %shard_map.113 = bf16[32,5120]{1,0:T(8,128)(2,1)} custom-call(bf16[32,80,128]{2,1,0:T(8,128)(2,1)} %copy-done), custom_call_target="tpu_custom_call" | custom-call | tf_op jit(solution)/shard_map/pallas_call | solution.py:39
  137.6 14.3 %all-to-all-done.2.refs_0_ = bf16[32,80,128]{2,1,0:T(8,128)(2,1)} async-done(((bf16[32,80,128]{2,1,0:T(8,128)(2,1)}), bf16[32,80,128]{2,1,0:T(8,128)(2,1)}, u32[]{:S(2)}, u32[]{:S(2)}) %all-to-all-start.2) | async-done | bytes 655392 | tf_op jit(solution)/shard_map/all_to_all | solution.py:335
  151.9 2.1 %shard_map.111 = bf16[32,5120]{1,0:T(8,128)(2,1)} custom-call(bf16[32,80,128]{2,1,0:T(8,128)(2,1)} %all-to-all-done.2.refs_0_, f32[1,5120]{1,0:T(1,128)} %constant_dynamic-slice_fusion.refs_1_), custom_call_target="tpu_custom_call" | custom-call | tf_op jit(solution)/shard_map/pallas_call | solution.py:39
  (49 shorter events, 18.1 us)
Async XLA Ops:
  3.0 42.7 %all-to-all-start = ((bf16[32,144,128]{2,1,0:T(8,128)(2,1)}), bf16[32,144,128]{2,1,0:T(8,128)(2,1)}, u32[]{:S(2)}, u32[]{:S(2)}) async-start(bf16[32,144,128]{2,1,0:T(8,128)(2,1)} %shard_map.104), calls=%async_computation | async-start | bytes 2359296 | tf_op jit(solution)/shard_map/all_to_all | solution.py:335
  14.8 2.6 %copy-start.1 = (s32[32]{0:T(128)S(1)}, s32[32]{0:T(128)}, u32[]{:S(2)}) copy-start(s32[32]{0:T(128)} %param.14) | copy-start | bytes 388
  17.4 2.3 %collective-permute-start = (bf16[2,1280,128]{2,1,0:T(8,128)(2,1)}, bf16[2,1280,128]{2,1,0:T(8,128)(2,1)S(1)}, u32[]{:S(2)}, u32[]{:S(2)}) collective-permute-start(bf16[2,1280,128]{2,1,0:T(8,128)(2,1)} %get-tuple-element.41), channel_id=1, source_target_pairs={{0,8},{8,0},{1,9},{9,1},{2,10},{10,2},{3,11},{11,3},{4,12},{12,4},... | collective-permute-start | bytes 1966088 | tf_op jit(solution)/shard_map/ppermute | solution.py:345
  19.8 10.5 %collective-permute-start.1 = (bf16[1280,128]{1,0:T(8,128)(2,1)S(1)}, bf16[1280,128]{1,0:T(8,128)(2,1)}, u32[]{:S(2)}, u32[]{:S(2)}) collective-permute-start(bf16[1280,128]{1,0:T(8,128)(2,1)S(1)} %dynamic-slice_bitcast_fusion), channel_id=1, source_target_pairs={{0,16},{16,0},{1,17},{17,1},{2,18},{18,2},{3,19},{19,3},{4,20},{20... | collective-permute-start | bytes 983048 | tf_op jit(solution)/shard_map/ppermute | solution.py:345
  23.4 25.8 %copy-start.3 = (s32[32]{0:T(128)S(1)}, s32[32]{0:T(128)}, u32[]{:S(2)}) copy-start(s32[32]{0:T(128)} %param.14) | copy-start | bytes 388
  23.4 25.9 %copy-start.5 = (s32[32]{0:T(128)S(1)}, s32[32]{0:T(128)}, u32[]{:S(2)}) copy-start(s32[32]{0:T(128)} %param.15) | copy-start | bytes 388
  47.7 17.6 %collective-permute-start.5 = (bf16[1280,128]{1,0:T(8,128)(2,1)S(1)}, bf16[1280,128]{1,0:T(8,128)(2,1)S(1)}, u32[]{:S(2)}, u32[]{:S(2)}) collective-permute-start(bf16[1280,128]{1,0:T(8,128)(2,1)S(1)} %bitcast_select_fusion), channel_id=1, source_target_pairs={{0,128},{32,160},{64,192},{96,224},{128,0},{160,32},{192,64},{224,... | collective-permute-start | bytes 983048 | tf_op jit(solution)/shard_map/ppermute | solution.py:345
  49.8 19.0 %collective-permute-start.2 = (bf16[32,80,128]{2,1,0:T(8,128)(2,1)}, bf16[32,80,128]{2,1,0:T(8,128)(2,1)}, u32[]{:S(2)}, u32[]{:S(2)}) collective-permute-start(bf16[32,80,128]{2,1,0:T(8,128)(2,1)} %slice.13.refs_1_), channel_id=1, source_target_pairs={{0,16},{16,4},{4,20},{20,0},{1,17},{17,5},{5,21},{21,1},{2,18},{18... | collective-permute-start | bytes 1966088 | tf_op jit(solution)/shard_map/ppermute | solution.py:340
  51.3 17.7 %collective-permute-start.3 = (bf16[32,80,128]{2,1,0:T(8,128)(2,1)}, bf16[32,80,128]{2,1,0:T(8,128)(2,1)}, u32[]{:S(2)}, u32[]{:S(2)}) collective-permute-start(bf16[32,80,128]{2,1,0:T(8,128)(2,1)} %slice.13.refs_1_), channel_id=1, source_target_pairs={{0,20},{16,0},{4,16},{20,4},{1,21},{17,1},{5,17},{21,5},{2,22},{18... | collective-permute-start | bytes 1966088 | tf_op jit(solution)/shard_map/ppermute | solution.py:340
  53.1 16.0 %collective-permute-start.4 = (bf16[32,80,128]{2,1,0:T(8,128)(2,1)}, bf16[32,80,128]{2,1,0:T(8,128)(2,1)}, u32[]{:S(2)}, u32[]{:S(2)}) collective-permute-start(bf16[32,80,128]{2,1,0:T(8,128)(2,1)} %slice.13.refs_1_), channel_id=1, source_target_pairs={{0,8},{8,0},{1,9},{9,1},{2,10},{10,2},{3,11},{11,3},{4,12},{12,4},... | collective-permute-start | bytes 1966088 | tf_op jit(solution)/shard_map/ppermute | solution.py:345
  54.3 35.8 %all-to-all-start.1 = ((bf16[32,64,128]{2,1,0:T(8,128)(2,1)}), bf16[32,64,128]{2,1,0:T(8,128)(2,1)}, u32[]{:S(2)}, u32[]{:S(2)}) async-start(bf16[32,64,128]{2,1,0:T(8,128)(2,1)} %shard_map.105), calls=%async_computation.1 | async-start | bytes 1048576 | tf_op jit(solution)/shard_map/all_to_all | solution.py:335
  70.8 19.4 %collective-permute-start.8 = (bf16[32,80,128]{2,1,0:T(8,128)(2,1)}, bf16[32,80,128]{2,1,0:T(8,128)(2,1)}, u32[]{:S(2)}, u32[]{:S(2)}) collective-permute-start(bf16[32,80,128]{2,1,0:T(8,128)(2,1)} %collective-permute-done.2.refs_2_), channel_id=1, source_target_pairs={{0,8},{8,0},{1,9},{9,1},{2,10},{10,2},{3,11},{11,3},{4,12},{12,4},... | collective-permute-start | bytes 1966088 | tf_op jit(solution)/shard_map/ppermute | solution.py:345
  72.5 17.7 %collective-permute-start.9 = (bf16[32,80,128]{2,1,0:T(8,128)(2,1)}, bf16[32,80,128]{2,1,0:T(8,128)(2,1)}, u32[]{:S(2)}, u32[]{:S(2)}) collective-permute-start(bf16[32,80,128]{2,1,0:T(8,128)(2,1)} %collective-permute-done.3.refs_3_), channel_id=1, source_target_pairs={{0,8},{8,0},{1,9},{9,1},{2,10},{10,2},{3,11},{11,3},{4,12},{12,4},... | collective-permute-start | bytes 1966088 | tf_op jit(solution)/shard_map/ppermute | solution.py:345
  73.0 17.1 %collective-permute-start.10 = (bf16[1280,128]{1,0:T(8,128)(2,1)S(1)}, bf16[1280,128]{1,0:T(8,128)(2,1)S(1)}, u32[]{:S(2)}, u32[]{:S(2)}) collective-permute-start(bf16[1280,128]{1,0:T(8,128)(2,1)S(1)} %broadcast_select_fusion.3), channel_id=1, source_target_pairs={{0,64},{32,96},{64,0},{96,32},{128,192},{160,224},{192,128},{224,1... | collective-permute-start | bytes 983048 | tf_op jit(solution)/shard_map/ppermute | solution.py:345
  75.8 14.4 %collective-permute-start.6 = (bf16[16,80,128]{2,1,0:T(8,128)(2,1)}, bf16[16,80,128]{2,1,0:T(8,128)(2,1)}, u32[]{:S(2)}, u32[]{:S(2)}) collective-permute-start(bf16[16,80,128]{2,1,0:T(8,128)(2,1)} %slice.14), channel_id=1, source_target_pairs={{0,16},{16,4},{4,20},{20,0},{1,17},{17,5},{5,21},{21,1},{2,18},{18... | collective-permute-start | bytes 983048 | tf_op jit(solution)/shard_map/ppermute | solution.py:340
  77.0 13.2 %collective-permute-start.7 = (bf16[16,80,128]{2,1,0:T(8,128)(2,1)}, bf16[16,80,128]{2,1,0:T(8,128)(2,1)}, u32[]{:S(2)}, u32[]{:S(2)}) collective-permute-start(bf16[16,80,128]{2,1,0:T(8,128)(2,1)} %slice.15), channel_id=1, source_target_pairs={{0,20},{16,0},{4,16},{20,4},{1,21},{17,1},{5,17},{21,5},{2,22},{18... | collective-permute-start | bytes 983048 | tf_op jit(solution)/shard_map/ppermute | solution.py:340
  90.2 9.7 %collective-permute-start.13 = (bf16[1280,128]{1,0:T(8,128)(2,1)S(1)}, bf16[1280,128]{1,0:T(8,128)(2,1)S(1)}, u32[]{:S(2)}, u32[]{:S(2)}) collective-permute-start(bf16[1280,128]{1,0:T(8,128)(2,1)S(1)} %broadcast_select_fusion.2), channel_id=1, source_target_pairs={{0,32},{32,0},{64,96},{96,64},{128,160},{160,128},{192,224},{224,1... | collective-permute-start | bytes 983048 | tf_op jit(solution)/shard_map/ppermute | solution.py:345
  90.3 10.4 %collective-permute-start.11 = (bf16[16,80,128]{2,1,0:T(8,128)(2,1)}, bf16[16,80,128]{2,1,0:T(8,128)(2,1)S(1)}, u32[]{:S(2)}, u32[]{:S(2)}) collective-permute-start(bf16[16,80,128]{2,1,0:T(8,128)(2,1)} %collective-permute-done.6.refs_3_), channel_id=1, source_target_pairs={{0,8},{8,0},{1,9},{9,1},{2,10},{10,2},{3,11},{11,3},{4,12},{12,4},... | collective-permute-start | bytes 983048 | tf_op jit(solution)/shard_map/ppermute | solution.py:345
  90.5 10.3 %collective-permute-start.12 = (bf16[16,80,128]{2,1,0:T(8,128)(2,1)}, bf16[16,80,128]{2,1,0:T(8,128)(2,1)}, u32[]{:S(2)}, u32[]{:S(2)}) collective-permute-start(bf16[16,80,128]{2,1,0:T(8,128)(2,1)} %collective-permute-done.7.refs_4_), channel_id=1, source_target_pairs={{0,8},{8,0},{1,9},{9,1},{2,10},{10,2},{3,11},{11,3},{4,12},{12,4},... | collective-permute-start | bytes 983048 | tf_op jit(solution)/shard_map/ppermute | solution.py:345
  100.7 3.9 %copy-start.4 = (bf16[16,80,128]{2,1,0:T(8,128)(2,1)}, bf16[16,80,128]{2,1,0:T(8,128)(2,1)S(1)}, u32[]{:S(2)}) copy-start(bf16[16,80,128]{2,1,0:T(8,128)(2,1)S(1)} %collective-permute-done.11.refs_1_) | copy-start | bytes 983044
  104.6 19.6 %all-to-all-start.3 = ((bf16[32,80,128]{2,1,0:T(8,128)(2,1)}), bf16[32,80,128]{2,1,0:T(8,128)(2,1)S(1)}, u32[]{:S(2)}, u32[]{:S(2)}) async-start(bf16[32,80,128]{2,1,0:T(8,128)(2,1)} %shard_map.112), calls=%async_computation.3 | async-start | bytes 1310720 | tf_op jit(solution)/shard_map/all_to_all | solution.py:335
  117.2 14.2 %copy-start.6 = (s32[32]{0:T(128)S(1)}, s32[32]{0:T(128)}, u32[]{:S(2)}) copy-start(s32[32]{0:T(128)} %param.16) | copy-start | bytes 388
  124.2 11.3 %copy-start = (bf16[32,80,128]{2,1,0:T(8,128)(2,1)}, bf16[32,80,128]{2,1,0:T(8,128)(2,1)S(1)}, u32[]{:S(2)}) copy-start(bf16[32,80,128]{2,1,0:T(8,128)(2,1)S(1)} %all-to-all-done.3.refs_0_) | copy-start | bytes 1966084
  124.2 27.6 %all-to-all-start.2 = ((bf16[32,80,128]{2,1,0:T(8,128)(2,1)}), bf16[32,80,128]{2,1,0:T(8,128)(2,1)}, u32[]{:S(2)}, u32[]{:S(2)}) async-start(bf16[32,80,128]{2,1,0:T(8,128)(2,1)} %shard_map.110), calls=%async_computation.2 | async-start | bytes 1310720 | tf_op jit(solution)/shard_map/all_to_all | solution.py:335
  (1 other events, 1.7 us)

commit v4 on v3

--- a/solution.py
+++ b/solution.py
@@ -384,7 +384,6 @@
     queries = exchange(blocks, COLUMN)
     queries, text_blocks, text = barrier((queries, text_blocks, text))
     own, text = barrier((queries[:, 64:144], text))
-    half = PEERS // 2
 
     up, down, other = shift(own, 1), shift(own, -1), swap(own, "core")
     text = text_along_z(text, 4, chosen)
@@ -392,7 +391,7 @@
     cross_queries = exchange(text_blocks, PLANE)
     up, down, other, text, state = barrier((up, down, other, text, state))
 
-    far = [shift(up[:half], 1), shift(down[half:], -1)]
+    far = shift(up, 1)
     other_up, other_down = swap(up, "core"), swap(down, "core")
     text = text_along_z(text, 2, chosen)
     state = self_step(queries, [other, up, down], state)
@@ -400,15 +399,15 @@
         (far, other_up, other_down, text, state, cross_queries)
     )
 
-    other_far = [swap(x, "core") for x in far]
+    other_far = swap(far, "core")
     text = text_along_z(text, 1, chosen)
-    state = self_step(queries, [other_up, other_down, *far], state)
+    state = self_step(queries, [other_up, other_down], state)
     other_far, text, state = barrier((other_far, text, state))
 
     place = lax.axis_index("xl") * 2 + lax.axis_index("core")
     cross = cross_step(jnp.stack([pick(text_lengths, chosen), place]), cross_queries, text)
     cross = exchange(cross, PLANE)
-    result = exchange(self_step(queries, other_far, state, last=True), COLUMN)
+    result = exchange(self_step(queries, [far, other_far], state, last=True), COLUMN)
     gate = lax.dynamic_slice_in_dim(time_gates, pick(timestep, chosen), 1, 0)
     return (unpack(self_slot, result, gate), unpack(cross_slot, cross))
 

time: 155 us -> 152 us (0.981)
  local copies, waits for them, and re-layouts: 8.18 us -> 4.75 us
  starting transfers between devices: 46.5 us -> 43.1 us
  waiting for transfers between devices: 52.7 us -> 55.5 us
  other arithmetic: 2.2 us -> 4.26 us
    ppermute x10 -> x9, waiting for transfers between devices: 12.4 us -> 16.1 us  [swap(): lax.ppermute(block, axis, [(at, at ^ distance) for at in range(size)])]
    slice x2 -> x0, local copies, waits for them, and re-layouts: 3.44 us -> none  [on_device(): far = [shift(up[:half], 1), shift(down[half:], -1)]]
    ppermute x4 -> x3, starting transfers between devices: 6.9 us -> 4.72 us  [shift(): return lax.ppermute(block, RING, pairs)]
    ppermute x10 -> x9, starting transfers between devices: 7.07 us -> 5.97 us  [swap(): lax.ppermute(block, axis, [(at, at ^ distance) for at in range(size)])]
    ppermute x4 -> x3, waiting for transfers between devices: 3.73 us -> 4.34 us  [shift(): return lax.ppermute(block, RING, pairs)]
  transfers between devices with their start and end apart: 18 -> 16, of which waited for: 9 -> 9; matrix products, arithmetic and copies ran while one was open for 5% -> 5% of each run, Pallas kernels for 21% -> 21%
where the time goes in v4:
time: 152 us; the launch traced here: 151 us
  waiting for transfers between devices  55.5 us (37%)
  starting transfers between devices  43.1 us (28%)
  Pallas kernels  40.7 us (27%)
  local copies, waits for them, and re-layouts  4.75 us (3%)
  other arithmetic  4.26 us (3%)
  between operations  3.02 us (2%)
    pallas_call x10, Pallas kernels, call(): pl.pallas_call(kernel, out_shape=out_shape, grid=(1,), in_specs=in_specs,...  40.7 us
    all_to_all x4, waiting for transfers between devices, exchange(): lax.all_to_all(messages, group, split_axis=0, concat_axis=0, tiled=True)  35.1 us
    all_to_all x4, starting transfers between devices, exchange(): lax.all_to_all(messages, group, split_axis=0, concat_axis=0, tiled=True)  32.4 us
    ppermute x9, waiting for transfers between devices, swap(): lax.ppermute(block, axis, [(at, at ^ distance) for at in range(size)])  16.1 us
    ppermute x9, starting transfers between devices, swap(): lax.ppermute(block, axis, [(at, at ^ distance) for at in range(size)])  5.97 us
    ppermute x3, starting transfers between devices, shift(): return lax.ppermute(block, RING, pairs)  4.72 us
    ppermute x3, waiting for transfers between devices, shift(): return lax.ppermute(block, RING, pairs)  4.34 us
  transfers between devices with their start and end apart: 16, of which 9 were waited for; matrix products, arithmetic and copies ran while one was open for 5% of the time, Pallas kernels for 21%

profile of v4, /device:TPU:8, one launch (start us, length us, event | category | flops | bytes accessed | tf_op | source)
XLA Modules:
  0.0 151.3 jit_solution(15449736804034941196)
XLA Ops:
  0.6 2.4 %shard_map.104 = bf16[32,144,128]{2,1,0:T(8,128)(2,1)} custom-call(bf16[32,5120]{1,0:T(8,128)(2,1)} %keys_ref.1, bf16[32,5120]{1,0:T(8,128)(2,1)} %values_ref.1, bf16[32,5120]{1,0:T(8,128)(2,1)} %queries_ref.2), custom_call_target="tpu_custom_call" | custom-call | tf_op jit(solution)/shard_map/pallas_call | solution.py:39
  3.0 11.7 %all-to-all-start = ((bf16[32,144,128]{2,1,0:T(8,128)(2,1)}), bf16[32,144,128]{2,1,0:T(8,128)(2,1)}, u32[]{:S(2)}, u32[]{:S(2)}) async-start(bf16[32,144,128]{2,1,0:T(8,128)(2,1)} %shard_map.104), calls=%async_computation | async-start | bytes 2359296 | tf_op jit(solution)/shard_map/all_to_all | solution.py:335
  14.8 2.6 %shard_map.106 = (bf16[2,1280,128]{2,1,0:T(8,128)(2,1)}, bf16[2,1280,128]{2,1,0:T(8,128)(2,1)}) custom-call(s32[1]{0:T(128)} %bitcast.1.core_ref, bf16[1,2,512,640]{3,2,1,0:T(8,128)(2,1)} %text_ref.1), custom_call_target="tpu_custom_call" | custom-call | tf_op jit(solution)/shard_map/pallas_call | solution.py:39
  17.5 2.2 %collective-permute-done = bf16[2,1280,128]{2,1,0:T(8,128)(2,1)S(1)} collective-permute-done((bf16[2,1280,128]{2,1,0:T(8,128)(2,1)}, bf16[2,1280,128]{2,1,0:T(8,128)(2,1)S(1)}, u32[]{:S(2)}, u32[]{:S(2)}) %collective-permute-start) | collective-permute-done | bytes 655392 | tf_op jit(solution)/shard_map/ppermute | solution.py:345
  22.6 1.9 %shard_map.105 = bf16[32,64,128]{2,1,0:T(8,128)(2,1)} custom-call(bf16[32,5120]{1,0:T(8,128)(2,1)} %queries_ref.3), custom_call_target="tpu_custom_call" | custom-call | tf_op jit(solution)/shard_map/pallas_call | solution.py:39
  24.4 5.3 %collective-permute-done.1 = bf16[1280,128]{1,0:T(8,128)(2,1)} collective-permute-done((bf16[1280,128]{1,0:T(8,128)(2,1)S(1)}, bf16[1280,128]{1,0:T(8,128)(2,1)}, u32[]{:S(2)}, u32[]{:S(2)}) %collective-permute-start.1) | collective-permute-done | bytes 327712 | tf_op jit(solution)/shard_map/ppermute | solution.py:345
  30.8 14.9 %all-to-all-done.refs_0_ = bf16[32,144,128]{2,1,0:T(8,128)(2,1)} async-done(((bf16[32,144,128]{2,1,0:T(8,128)(2,1)}), bf16[32,144,128]{2,1,0:T(8,128)(2,1)}, u32[]{:S(2)}, u32[]{:S(2)}) %all-to-all-start) | async-done | bytes 1179680 | tf_op jit(solution)/shard_map/all_to_all | solution.py:335
  45.7 2.0 %slice.7.refs_1_ = bf16[32,80,128]{2,1,0:T(8,128)(2,1)} slice(bf16[32,144,128]{2,1,0:T(8,128)(2,1)} %all-to-all-done.refs_0_), slice={[0:32], [64:144], [0:128]} | slice | bytes 1310720 | tf_op jit(solution)/shard_map/slice | solution.py:386
  50.6 1.7 %collective-permute-start.3 = (bf16[32,80,128]{2,1,0:T(8,128)(2,1)}, bf16[32,80,128]{2,1,0:T(8,128)(2,1)}, u32[]{:S(2)}, u32[]{:S(2)}) collective-permute-start(bf16[32,80,128]{2,1,0:T(8,128)(2,1)} %slice.7.refs_1_), channel_id=1, source_target_pairs={{0,20},{16,0},{4,16},{20,4},{1,21},{17,1},{5,17},{21,5},{2,22},{18... | collective-permute-start | bytes 1966088 | tf_op jit(solution)/shard_map/ppermute | solution.py:340
  53.1 6.1 %all-to-all-start.1 = ((bf16[32,64,128]{2,1,0:T(8,128)(2,1)}), bf16[32,64,128]{2,1,0:T(8,128)(2,1)}, u32[]{:S(2)}, u32[]{:S(2)}) async-start(bf16[32,64,128]{2,1,0:T(8,128)(2,1)} %shard_map.105), calls=%async_computation.1 | async-start | bytes 1048576 | tf_op jit(solution)/shard_map/all_to_all | solution.py:335
  59.1 4.8 %shard_map.107 = (f32[1024,128]{1,0:T(8,128)}, f32[1024,128]{1,0:T(8,128)}, f32[1024,128]{1,0:T(8,128)}) custom-call(bf16[32,144,128]{2,1,0:T(8,128)(2,1)} %all-to-all-done.refs_0_, bf16[32,80,128]{2,1,0:T(8,128)(2,1)} %slice.7.refs_1_), custom_call_target="tpu_custom_call" | custom-call | flops 1342177280 | bytes 2752512 | tf_op jit(solution)/shard_map/pallas_call | solution.py:39
  64.0 4.2 %collective-permute-done.2.refs_2_ = bf16[32,80,128]{2,1,0:T(8,128)(2,1)} collective-permute-done((bf16[32,80,128]{2,1,0:T(8,128)(2,1)}, bf16[32,80,128]{2,1,0:T(8,128)(2,1)}, u32[]{:S(2)}, u32[]{:S(2)}) %collective-permute-start.2) | collective-permute-done | bytes 655392 | tf_op jit(solution)/shard_map/ppermute | solution.py:340
  69.8 2.5 %collective-permute-start.9 = (bf16[1280,128]{1,0:T(8,128)(2,1)S(1)}, bf16[1280,128]{1,0:T(8,128)(2,1)S(1)}, u32[]{:S(2)}, u32[]{:S(2)}) collective-permute-start(bf16[1280,128]{1,0:T(8,128)(2,1)S(1)} %broadcast_select_fusion.3), channel_id=1, source_target_pairs={{0,64},{32,96},{64,0},{96,32},{128,192},{160,224},{192,128},{224,1... | collective-permute-start | bytes 983048 | tf_op jit(solution)/shard_map/ppermute | solution.py:345
  72.6 8.2 %shard_map.108 = (f32[1024,128]{1,0:T(8,128)}, f32[1024,128]{1,0:T(8,128)}, f32[1024,128]{1,0:T(8,128)}) custom-call(bf16[32,144,128]{2,1,0:T(8,128)(2,1)} %all-to-all-done.refs_0_, bf16[32,80,128]{2,1,0:T(8,128)(2,1)} %collective-permute-done.4.refs_1_, bf16[32,80,128]{2,1,0:T(8,128)(2,1)} %collective-permute-done.2.refs_2_, ...), custom_call_target="tpu_custom_call" | custom-call | flops 4026531840 | bytes 4063232 | tf_op jit(solution)/shard_map/pallas_call | solution.py:39
  80.7 6.9 %collective-permute-done.9 = bf16[1280,128]{1,0:T(8,128)(2,1)S(1)} collective-permute-done((bf16[1280,128]{1,0:T(8,128)(2,1)S(1)}, bf16[1280,128]{1,0:T(8,128)(2,1)S(1)}, u32[]{:S(2)}, u32[]{:S(2)}) %collective-permute-start.9) | collective-permute-done | bytes 327712 | tf_op jit(solution)/shard_map/ppermute | solution.py:345
  89.2 6.7 %shard_map.109 = (f32[1024,128]{1,0:T(8,128)}, f32[1024,128]{1,0:T(8,128)}, f32[1024,128]{1,0:T(8,128)}) custom-call(bf16[32,144,128]{2,1,0:T(8,128)(2,1)} %all-to-all-done.refs_0_, bf16[32,80,128]{2,1,0:T(8,128)(2,1)} %collective-permute-done.7.refs_1_, bf16[32,80,128]{2,1,0:T(8,128)(2,1)} %collective-permute-done.8.refs_2_, ...), custom_call_target="tpu_custom_call" | custom-call | flops 2684354560 | bytes 3407872 | tf_op jit(solution)/shard_map/pallas_call | solution.py:39
  98.3 3.8 %shard_map.112 = bf16[32,80,128]{2,1,0:T(8,128)(2,1)} custom-call(s32[2]{0:T(128)} %pad_add_fusion.scalars_ref, bf16[32,64,128]{2,1,0:T(8,128)(2,1)} %all-to-all-done.1.queries_ref, bf16[1280,128]{1,0:T(8,128)(2,1)} %broadcast_select_fusion.1.text_ref), custom_call_target="tpu_custom_call" | custom-call | flops 671088640 | bytes 2097152 | tf_op jit(solution)/shard_map/pallas_call | solution.py:39
  102.1 7.3 %all-to-all-start.3 = ((bf16[32,80,128]{2,1,0:T(8,128)(2,1)}), bf16[32,80,128]{2,1,0:T(8,128)(2,1)S(1)}, u32[]{:S(2)}, u32[]{:S(2)}) async-start(bf16[32,80,128]{2,1,0:T(8,128)(2,1)} %shard_map.112), calls=%async_computation.3 | async-start | bytes 1310720 | tf_op jit(solution)/shard_map/all_to_all | solution.py:335
  109.4 6.2 %shard_map.110 = bf16[32,80,128]{2,1,0:T(8,128)(2,1)} custom-call(bf16[32,144,128]{2,1,0:T(8,128)(2,1)} %all-to-all-done.refs_0_, bf16[32,80,128]{2,1,0:T(8,128)(2,1)} %collective-permute-done.6.refs_1_, bf16[32,80,128]{2,1,0:T(8,128)(2,1)} %collective-permute-done.10.refs_2_, f32[1024,128]{1,0:T(8,128)} %get-tuple-element.69.refs_3_, ...), custom_call_target="tpu_custom_call" | custom-call | flops 2684354560 | bytes 3407872 | tf_op jit(solution)/shard_map/pallas_call | solution.py:39
  115.5 5.9 %all-to-all-done.3.refs_0_ = bf16[32,80,128]{2,1,0:T(8,128)(2,1)S(1)} async-done(((bf16[32,80,128]{2,1,0:T(8,128)(2,1)}), bf16[32,80,128]{2,1,0:T(8,128)(2,1)S(1)}, u32[]{:S(2)}, u32[]{:S(2)}) %all-to-all-start.3) | async-done | bytes 655392 | tf_op jit(solution)/shard_map/all_to_all | solution.py:335
  121.4 7.3 %all-to-all-start.2 = ((bf16[32,80,128]{2,1,0:T(8,128)(2,1)}), bf16[32,80,128]{2,1,0:T(8,128)(2,1)}, u32[]{:S(2)}, u32[]{:S(2)}) async-start(bf16[32,80,128]{2,1,0:T(8,128)(2,1)} %shard_map.110), calls=%async_computation.2 | async-start | bytes 1310720 | tf_op jit(solution)/shard_map/all_to_all | solution.py:335
  132.8 2.1 %shard_map.113 = bf16[32,5120]{1,0:T(8,128)(2,1)} custom-call(bf16[32,80,128]{2,1,0:T(8,128)(2,1)} %copy-done), custom_call_target="tpu_custom_call" | custom-call | tf_op jit(solution)/shard_map/pallas_call | solution.py:39
  134.9 14.2 %all-to-all-done.2.refs_0_ = bf16[32,80,128]{2,1,0:T(8,128)(2,1)} async-done(((bf16[32,80,128]{2,1,0:T(8,128)(2,1)}), bf16[32,80,128]{2,1,0:T(8,128)(2,1)}, u32[]{:S(2)}, u32[]{:S(2)}) %all-to-all-start.2) | async-done | bytes 655392 | tf_op jit(solution)/shard_map/all_to_all | solution.py:335
  149.1 2.1 %shard_map.111 = bf16[32,5120]{1,0:T(8,128)(2,1)} custom-call(bf16[32,80,128]{2,1,0:T(8,128)(2,1)} %all-to-all-done.2.refs_0_, f32[1,5120]{1,0:T(1,128)} %constant_dynamic-slice_fusion.refs_1_), custom_call_target="tpu_custom_call" | custom-call | tf_op jit(solution)/shard_map/pallas_call | solution.py:39
  (41 shorter events, 15.3 us)
Async XLA Ops:
  3.0 42.7 %all-to-all-start = ((bf16[32,144,128]{2,1,0:T(8,128)(2,1)}), bf16[32,144,128]{2,1,0:T(8,128)(2,1)}, u32[]{:S(2)}, u32[]{:S(2)}) async-start(bf16[32,144,128]{2,1,0:T(8,128)(2,1)} %shard_map.104), calls=%async_computation | async-start | bytes 2359296 | tf_op jit(solution)/shard_map/all_to_all | solution.py:335
  14.8 2.6 %copy-start.1 = (s32[32]{0:T(128)S(1)}, s32[32]{0:T(128)}, u32[]{:S(2)}) copy-start(s32[32]{0:T(128)} %param.14) | copy-start | bytes 388
  17.4 2.3 %collective-permute-start = (bf16[2,1280,128]{2,1,0:T(8,128)(2,1)}, bf16[2,1280,128]{2,1,0:T(8,128)(2,1)S(1)}, u32[]{:S(2)}, u32[]{:S(2)}) collective-permute-start(bf16[2,1280,128]{2,1,0:T(8,128)(2,1)} %get-tuple-element.39), channel_id=1, source_target_pairs={{0,8},{8,0},{1,9},{9,1},{2,10},{10,2},{3,11},{11,3},{4,12},{12,4},... | collective-permute-start | bytes 1966088 | tf_op jit(solution)/shard_map/ppermute | solution.py:345
  19.7 2.8 %copy-start.2 = (s32[32]{0:T(128)S(1)}, s32[32]{0:T(128)}, u32[]{:S(2)}) copy-start(s32[32]{0:T(128)} %param.14) | copy-start | bytes 388
  20.9 8.8 %collective-permute-start.1 = (bf16[1280,128]{1,0:T(8,128)(2,1)S(1)}, bf16[1280,128]{1,0:T(8,128)(2,1)}, u32[]{:S(2)}, u32[]{:S(2)}) collective-permute-start(bf16[1280,128]{1,0:T(8,128)(2,1)S(1)} %dynamic-slice_bitcast_fusion), channel_id=1, source_target_pairs={{0,16},{16,0},{1,17},{17,1},{2,18},{18,2},{3,19},{19,3},{4,20},{20... | collective-permute-start | bytes 983048 | tf_op jit(solution)/shard_map/ppermute | solution.py:345
  24.4 27.9 %copy-start.3 = (s32[32]{0:T(128)S(1)}, s32[32]{0:T(128)}, u32[]{:S(2)}) copy-start(s32[32]{0:T(128)} %param.14) | copy-start | bytes 388
  24.4 28.0 %copy-start.4 = (s32[32]{0:T(128)S(1)}, s32[32]{0:T(128)}, u32[]{:S(2)}) copy-start(s32[32]{0:T(128)} %param.15) | copy-start | bytes 388
  47.7 16.3 %collective-permute-start.5 = (bf16[1280,128]{1,0:T(8,128)(2,1)S(1)}, bf16[1280,128]{1,0:T(8,128)(2,1)S(1)}, u32[]{:S(2)}, u32[]{:S(2)}) collective-permute-start(bf16[1280,128]{1,0:T(8,128)(2,1)S(1)} %bitcast_select_fusion), channel_id=1, source_target_pairs={{0,128},{32,160},{64,192},{96,224},{128,0},{160,32},{192,64},{224,... | collective-permute-start | bytes 983048 | tf_op jit(solution)/shard_map/ppermute | solution.py:345
  49.1 19.0 %collective-permute-start.2 = (bf16[32,80,128]{2,1,0:T(8,128)(2,1)}, bf16[32,80,128]{2,1,0:T(8,128)(2,1)}, u32[]{:S(2)}, u32[]{:S(2)}) collective-permute-start(bf16[32,80,128]{2,1,0:T(8,128)(2,1)} %slice.7.refs_1_), channel_id=1, source_target_pairs={{0,16},{16,4},{4,20},{20,0},{1,17},{17,5},{5,21},{21,1},{2,18},{18... | collective-permute-start | bytes 1966088 | tf_op jit(solution)/shard_map/ppermute | solution.py:340
  50.6 17.7 %collective-permute-start.3 = (bf16[32,80,128]{2,1,0:T(8,128)(2,1)}, bf16[32,80,128]{2,1,0:T(8,128)(2,1)}, u32[]{:S(2)}, u32[]{:S(2)}) collective-permute-start(bf16[32,80,128]{2,1,0:T(8,128)(2,1)} %slice.7.refs_1_), channel_id=1, source_target_pairs={{0,20},{16,0},{4,16},{20,4},{1,21},{17,1},{5,17},{21,5},{2,22},{18... | collective-permute-start | bytes 1966088 | tf_op jit(solution)/shard_map/ppermute | solution.py:340
  52.4 16.0 %collective-permute-start.4 = (bf16[32,80,128]{2,1,0:T(8,128)(2,1)}, bf16[32,80,128]{2,1,0:T(8,128)(2,1)}, u32[]{:S(2)}, u32[]{:S(2)}) collective-permute-start(bf16[32,80,128]{2,1,0:T(8,128)(2,1)} %slice.7.refs_1_), channel_id=1, source_target_pairs={{0,8},{8,0},{1,9},{9,1},{2,10},{10,2},{3,11},{11,3},{4,12},{12,4},... | collective-permute-start | bytes 1966088 | tf_op jit(solution)/shard_map/ppermute | solution.py:345
  53.1 34.7 %all-to-all-start.1 = ((bf16[32,64,128]{2,1,0:T(8,128)(2,1)}), bf16[32,64,128]{2,1,0:T(8,128)(2,1)}, u32[]{:S(2)}, u32[]{:S(2)}) async-start(bf16[32,64,128]{2,1,0:T(8,128)(2,1)} %shard_map.105), calls=%async_computation.1 | async-start | bytes 1048576 | tf_op jit(solution)/shard_map/all_to_all | solution.py:335
  68.3 19.4 %collective-permute-start.6 = (bf16[32,80,128]{2,1,0:T(8,128)(2,1)}, bf16[32,80,128]{2,1,0:T(8,128)(2,1)}, u32[]{:S(2)}, u32[]{:S(2)}) collective-permute-start(bf16[32,80,128]{2,1,0:T(8,128)(2,1)} %collective-permute-done.2.refs_2_), channel_id=1, source_target_pairs={{0,16},{16,4},{4,20},{20,0},{1,17},{17,5},{5,21},{21,1},{2,18},{18... | collective-permute-start | bytes 1966088 | tf_op jit(solution)/shard_map/ppermute | solution.py:340
  69.8 17.9 %collective-permute-start.7 = (bf16[32,80,128]{2,1,0:T(8,128)(2,1)}, bf16[32,80,128]{2,1,0:T(8,128)(2,1)}, u32[]{:S(2)}, u32[]{:S(2)}) collective-permute-start(bf16[32,80,128]{2,1,0:T(8,128)(2,1)} %collective-permute-done.2.refs_2_), channel_id=1, source_target_pairs={{0,8},{8,0},{1,9},{9,1},{2,10},{10,2},{3,11},{11,3},{4,12},{12,4},... | collective-permute-start | bytes 1966088 | tf_op jit(solution)/shard_map/ppermute | solution.py:345
  69.8 17.8 %collective-permute-start.9 = (bf16[1280,128]{1,0:T(8,128)(2,1)S(1)}, bf16[1280,128]{1,0:T(8,128)(2,1)S(1)}, u32[]{:S(2)}, u32[]{:S(2)}) collective-permute-start(bf16[1280,128]{1,0:T(8,128)(2,1)S(1)} %broadcast_select_fusion.3), channel_id=1, source_target_pairs={{0,64},{32,96},{64,0},{96,32},{128,192},{160,224},{192,128},{224,1... | collective-permute-start | bytes 983048 | tf_op jit(solution)/shard_map/ppermute | solution.py:345
  72.4 15.4 %collective-permute-start.8 = (bf16[32,80,128]{2,1,0:T(8,128)(2,1)}, bf16[32,80,128]{2,1,0:T(8,128)(2,1)}, u32[]{:S(2)}, u32[]{:S(2)}) collective-permute-start(bf16[32,80,128]{2,1,0:T(8,128)(2,1)} %collective-permute-done.3.refs_3_), channel_id=1, source_target_pairs={{0,8},{8,0},{1,9},{9,1},{2,10},{10,2},{3,11},{11,3},{4,12},{12,4},... | collective-permute-start | bytes 1966088 | tf_op jit(solution)/shard_map/ppermute | solution.py:345
  87.8 9.8 %collective-permute-start.11 = (bf16[1280,128]{1,0:T(8,128)(2,1)S(1)}, bf16[1280,128]{1,0:T(8,128)(2,1)S(1)}, u32[]{:S(2)}, u32[]{:S(2)}) collective-permute-start(bf16[1280,128]{1,0:T(8,128)(2,1)S(1)} %broadcast_select_fusion.2), channel_id=1, source_target_pairs={{0,32},{32,0},{64,96},{96,64},{128,160},{160,128},{192,224},{224,1... | collective-permute-start | bytes 983048 | tf_op jit(solution)/shard_map/ppermute | solution.py:345
  89.1 9.2 %collective-permute-start.10 = (bf16[32,80,128]{2,1,0:T(8,128)(2,1)}, bf16[32,80,128]{2,1,0:T(8,128)(2,1)}, u32[]{:S(2)}, u32[]{:S(2)}) collective-permute-start(bf16[32,80,128]{2,1,0:T(8,128)(2,1)} %collective-permute-done.6.refs_1_), channel_id=1, source_target_pairs={{0,8},{8,0},{1,9},{9,1},{2,10},{10,2},{3,11},{11,3},{4,12},{12,4},... | collective-permute-start | bytes 1966088 | tf_op jit(solution)/shard_map/ppermute | solution.py:345
  102.1 19.4 %all-to-all-start.3 = ((bf16[32,80,128]{2,1,0:T(8,128)(2,1)}), bf16[32,80,128]{2,1,0:T(8,128)(2,1)S(1)}, u32[]{:S(2)}, u32[]{:S(2)}) async-start(bf16[32,80,128]{2,1,0:T(8,128)(2,1)} %shard_map.112), calls=%async_computation.3 | async-start | bytes 1310720 | tf_op jit(solution)/shard_map/all_to_all | solution.py:335
  115.5 13.2 %copy-start.5 = (s32[32]{0:T(128)S(1)}, s32[32]{0:T(128)}, u32[]{:S(2)}) copy-start(s32[32]{0:T(128)} %param.16) | copy-start | bytes 388
  121.4 11.4 %copy-start = (bf16[32,80,128]{2,1,0:T(8,128)(2,1)}, bf16[32,80,128]{2,1,0:T(8,128)(2,1)S(1)}, u32[]{:S(2)}) copy-start(bf16[32,80,128]{2,1,0:T(8,128)(2,1)S(1)} %all-to-all-done.3.refs_0_) | copy-start | bytes 1966084
  121.4 27.7 %all-to-all-start.2 = ((bf16[32,80,128]{2,1,0:T(8,128)(2,1)}), bf16[32,80,128]{2,1,0:T(8,128)(2,1)}, u32[]{:S(2)}, u32[]{:S(2)}) async-start(bf16[32,80,128]{2,1,0:T(8,128)(2,1)} %shard_map.110), calls=%async_computation.2 | async-start | bytes 1310720 | tf_op jit(solution)/shard_map/all_to_all | solution.py:335
